TPU v7x, 512 devices: a whole 4x4x16 slice. The times are simulated.
512 devices in a mesh: gx: 32 (over z, core), gy: 16 (over x, y).
Axes of the slice: x: 4, y: 4, z: 16, core: 2. Of those that a mesh axis runs over, the one named last changes fastest.
Arguments:
- send_owner: int32 [32, 16, 32], P('gx', 'gy'), may hold values from 0 to 16, as said below
- send_box: int32 [32, 16, 32], P('gx', 'gy'), may hold values from 0 to 3, as said below
- rho_old: float32 [32, 16, 32, 8, 1024], P('gx', 'gy'), may hold values from 0.15 to 1.2
- rhs_old: float32 [32, 16, 32, 8, 1024], P('gx', 'gy'), may hold values from -6 to 6
Outputs:
- phi: float32 [8, 1024, 2048], P(None, 'gx', 'gy')
Inputs may be any that keep to these rules, and one draw needn't show every extreme that they name: `send_owner`: in each gx row, every box of every new owner is named by exactly one slot; no old owner gives more than 2 boxes to one new owner, and in every row one old owner gives exactly 2 to every new owner. 16 marks an empty slot. `send_box`: empty slots hold 0.
All inputs are finite; a program needn't handle non-finite values.
Results may differ from a plain program's by a relative error of at most 0.00027.
Values sent between devices are 32-bit elements; how exact they have to be, the bound alone decides.
A program may use at most 128 MiB of HBM per device.

v0:
```python
import jax
import jax.numpy as jnp
from jax import lax
from jax.sharding import PartitionSpec as P

CX = 32
CY = 128
BS = 32
BOTTOM = 6
CYCLES = 2
BOX_DEV = 4


def padded_2(x, sides, width):
    for axis, dim in sides:
        devices, length = (lax.axis_size(axis), x.shape[dim])
        up = [(i, (i + 1) % devices) for i in range(devices - 1)]
        down = [(j, i) for i, j in up]
        last = lax.slice_in_dim(x, length - width, length, axis=dim)
        first = lax.slice_in_dim(x, 0, width, axis=dim)
        before = lax.ppermute(last, axis, up)
        after = lax.ppermute(first, axis, down)
        x = jnp.concatenate([before, x, after], axis=dim)
    return x


def restrict_mean(field):
    extent = field.shape
    return field.reshape(extent[0] // 2, 2, extent[1] // 2, 2, extent[2] // 2, 2).mean(
        axis=(1, 3, 5)
    )


def prolong_copy(coarse):
    extent = coarse.shape
    wide = jnp.broadcast_to(
        coarse[:, None, :, None, :, None], (extent[0], 2, extent[1], 2, extent[2], 2)
    )
    return wide.reshape(2 * extent[0], 2 * extent[1], 2 * extent[2])


def face_weights(padded):
    centre = padded[1:-1, 1:-1, 1:-1]
    to_east = (centre + padded[2:, 1:-1, 1:-1]) * 0.5
    to_west = (padded[:-2, 1:-1, 1:-1] + centre) * 0.5
    to_north = (centre + padded[1:-1, 2:, 1:-1]) * 0.5
    to_south = (padded[1:-1, :-2, 1:-1] + centre) * 0.5
    to_upper = (centre + padded[1:-1, 1:-1, 2:]) * 0.5
    to_lower = (padded[1:-1, 1:-1, :-2] + centre) * 0.5
    return (to_east, to_west, to_north, to_south, to_upper, to_lower)


def neighbour_sum(padded, weights):
    summed = weights[0] * padded[2:, 1:-1, 1:-1] + weights[1] * padded[:-2, 1:-1, 1:-1]
    summed = summed + weights[2] * padded[1:-1, 2:, 1:-1] + weights[3] * padded[1:-1, :-2, 1:-1]
    summed = summed + weights[4] * padded[1:-1, 1:-1, 2:] + weights[5] * padded[1:-1, 1:-1, :-2]
    return summed


def make_level(padded, weight_scale):
    weights = face_weights(padded)
    summed = weights[0] + weights[1]
    summed = summed + weights[2] + weights[3]
    summed = summed + weights[4] + weights[5]
    return (weights, weight_scale * summed, weight_scale)


def colour_mask(extent):
    index_x = jnp.arange(extent[0], dtype=jnp.int32)
    index_y = jnp.arange(extent[1], dtype=jnp.int32)
    index_z = jnp.arange(extent[2], dtype=jnp.int32)
    return (index_x[:, None, None] + index_y[None, :, None] + index_z[None, None, :]) % 2


def smooth(field, source, level_data, pad_fn, parity):
    weights, diagonal, weight_scale = level_data
    for colour in (0, 1):
        summed = neighbour_sum(pad_fn(field), weights)
        field = jnp.where(parity == colour, (source + weight_scale * summed) / diagonal, field)
    return field


def residual_of(field, source, level_data, pad_fn):
    weights, diagonal, weight_scale = level_data
    summed = neighbour_sum(pad_fn(field), weights)
    return source - (diagonal * field - weight_scale * summed)


def pad_cells(field):
    padded = padded_2(field, (("gx", 1), ("gy", 2)), 1)
    return jnp.pad(padded, ((1, 1), (0, 0), (0, 0)))


def pad_density(field):
    padded = padded_2(field, (("gx", 1), ("gy", 2)), 1)
    return jnp.pad(padded, ((1, 1), (0, 0), (0, 0)))


def local(send_owner, send_box, rho_old, rhs_old):
    groups = lax.axis_size("gy")
    slot_count = send_owner.shape[2]
    capacity = slot_count // groups
    depth = rho_old.shape[3]
    cell_count = rho_old.shape[4]
    owner_list = send_owner.reshape(slot_count)
    box_list = send_box.reshape(slot_count)
    hits = (owner_list[:, None] == jnp.arange(groups, dtype=jnp.int32)[None, :]).astype(jnp.int32)
    running = jnp.cumsum(hits, axis=0) - 1
    own_rank = jnp.sum(hits * running, axis=1)
    position = jnp.where(owner_list < groups, owner_list * capacity + own_rank, groups * capacity)
    match = position[None, :] == jnp.arange(groups * capacity, dtype=jnp.int32)[:, None]
    filled = jnp.any(match, axis=1)
    source_slot = jnp.sum(
        jnp.where(match, jnp.arange(slot_count, dtype=jnp.int32)[None, :], 0), axis=1
    )
    box_ids = jnp.where(filled, jnp.sum(jnp.where(match, box_list[None, :], 0), axis=1), -1)
    rho_boxes = rho_old.reshape(slot_count, depth, cell_count)
    rhs_boxes = rhs_old.reshape(slot_count, depth, cell_count)
    rho_buffer = jnp.where(filled[:, None, None], jnp.take(rho_boxes, source_slot, axis=0), 0.0)
    rhs_buffer = jnp.where(filled[:, None, None], jnp.take(rhs_boxes, source_slot, axis=0), 0.0)
    rho_buffer = rho_buffer.reshape(groups, capacity, depth, cell_count)
    rhs_buffer = rhs_buffer.reshape(groups, capacity, depth, cell_count)
    id_buffer = box_ids.reshape(groups, capacity)
    rho_in, rhs_in, ids_in = (
        lax.all_to_all(rho_buffer, "gy", split_axis=0, concat_axis=0, tiled=True),
        lax.all_to_all(rhs_buffer, "gy", split_axis=0, concat_axis=0, tiled=True),
        lax.all_to_all(id_buffer, "gy", split_axis=0, concat_axis=0, tiled=True),
    )
    pick = ids_in.reshape(-1)[None, :] == jnp.arange(BOX_DEV, dtype=jnp.int32)[:, None]
    from_slot = jnp.sum(
        jnp.where(pick, jnp.arange(groups * capacity, dtype=jnp.int32)[None, :], 0), axis=1
    )

    def assemble(incoming):
        box_data = jnp.take(
            incoming.reshape(groups * capacity, depth, cell_count), from_slot, axis=0
        )
        box_data = box_data.reshape(CX // BS, CY // BS, depth, BS, BS)
        return box_data.transpose(2, 0, 3, 1, 4).reshape(depth, CX, CY)

    density = assemble(rho_in)
    source = assemble(rhs_in)
    inverse_fine = 1.0 / density
    inverse_mid = restrict_mean(inverse_fine)
    inverse_coarse = restrict_mean(inverse_mid)
    level_fine = make_level(pad_density(inverse_fine), 1.0)
    level_mid = make_level(pad_density(inverse_mid), 0.25)
    parity_fine = colour_mask(inverse_fine.shape)
    parity_mid = colour_mask(inverse_mid.shape)
    level_coarse = make_level(pad_density(inverse_coarse), 0.0625)
    parity_coarse = colour_mask(inverse_coarse.shape)
    field = jnp.zeros_like(source)
    for cycle_step in range(CYCLES):
        field = smooth(field, source, level_fine, pad_cells, parity_fine)
        source_mid = restrict_mean(residual_of(field, source, level_fine, pad_cells))
        field_mid = smooth(jnp.zeros_like(source_mid), source_mid, level_mid, pad_cells, parity_mid)
        source_coarse = restrict_mean(residual_of(field_mid, source_mid, level_mid, pad_cells))
        field_coarse = jnp.zeros_like(source_coarse)
        for sweep_step in range(BOTTOM):
            field_coarse = smooth(
                field_coarse, source_coarse, level_coarse, pad_cells, parity_coarse
            )
        field_mid = smooth(
            field_mid + prolong_copy(field_coarse), source_mid, level_mid, pad_cells, parity_mid
        )
        field = smooth(field + prolong_copy(field_mid), source, level_fine, pad_cells, parity_fine)
    return field


def solution(mesh):
    placed = (
        P("gx", "gy", None),
        P("gx", "gy", None),
        P("gx", "gy", None, None, None),
        P("gx", "gy", None, None, None),
    )
    return jax.shard_map(
        local, mesh=mesh, in_specs=placed, out_specs=P(None, "gx", "gy"), check_vma=False
    )
```

profile of v0, /device:TPU:125, one launch (start us, length us, event | category | flops | bytes accessed | tf_op | source)
XLA Modules:
  0.0 922.9 jit_solution(1486647647393188710)
XLA Ops:
  0.0 5.4 collective-permute-start.4
  7.4 4.9 collective-permute-start.36
  18.1 6.6 all-to-all-start.1
  24.6 5.4 collective-permute-start.20
  34.2 6.7 all-to-all-start
  52.6 7.1 all-to-all-start.2
  65.8 6.4 collective-permute-done.22
  82.5 4.4 collective-permute-done.7
  90.0 6.1 div.173
  139.6 5.5 collective-permute-start.18
  156.7 5.8 collective-permute-start.14
  165.0 5.6 collective-permute-done.15
  171.2 9.7 %reshape.177 = f32[4,2,16,2,64,2]{5,4,3,2,1,0:T(8,128)} reshape(f32[8,32,128]{2,1,0:T(8,128)S(1)} %fusion.97) | data formatting | bytes 262144 | tf_op jit(solution)/shard_map/reshape | solution.py:29
  190.5 4.9 collective-permute-start.32
  206.6 6.0 collective-permute-start.28
  226.1 4.8 collective-permute-done.31
  232.7 6.6 collective-permute-start.40
  241.2 4.2 collective-permute-done.41
  295.2 4.2 collective-permute-done.53
  313.2 4.2 collective-permute-done.57
  367.2 4.2 collective-permute-done.69
  385.3 4.2 collective-permute-done.73
  475.8 6.9 reshape.180
  487.8 4.2 collective-permute-done.93
  507.9 4.2 collective-permute-done.97
  528.0 4.2 collective-permute-done.101
  548.1 4.2 collective-permute-done.105
  568.1 4.2 collective-permute-done.109
  583.1 9.7 %reshape.181 = f32[4,2,16,2,64,2]{5,4,3,2,1,0:T(8,128)} reshape(f32[8,32,128]{2,1,0:T(8,128)S(1)} %fusion.38) | data formatting | bytes 262144 | tf_op jit(solution)/shard_map/reshape | solution.py:29
  875.0 6.9 reshape.184
  886.9 4.2 collective-permute-done.173
  907.0 4.2 collective-permute-done.177
  (690 shorter events, 743.4 us)
Async XLA Ops:
  0.0 75.4 %collective-permute-start.4 = (f32[8,1,128]{2,1,0:T(1,128)S(1)}, f32[8,1,128]{2,1,0:T(1,128)S(1)}, u32[]{:S(2)}, u32[]{:S(2)}) collective-permute-start(f32[8,1,128]{2,1,0:T(1,128)S(1)} %broadcast.268), channel_id=1, source_target_pairs={{0,16},{16,32},{32,48},{48,64},{64,80},{80,96},{96,112},{112,128},... | collective-permute-start | bytes 12296 | tf_op jit(solution)/shard_map/ppermute | solution.py:21
  5.5 70.0 %collective-permute-start.5 = (f32[8,1,128]{2,1,0:T(1,128)S(1)}, f32[8,1,128]{2,1,0:T(1,128)S(1)}, u32[]{:S(2)}, u32[]{:S(2)}) collective-permute-start(f32[8,1,128]{2,1,0:T(1,128)S(1)} %broadcast.268), channel_id=1, source_target_pairs={{16,0},{32,16},{48,32},{64,48},{80,64},{96,80},{112,96},{128,112},... | collective-permute-start | bytes 12296 | tf_op jit(solution)/shard_map/ppermute | solution.py:22
  7.4 34.9 %collective-permute-start.36 = (f32[2,1,32]{2,1,0:T(1,128)S(1)}, f32[2,1,32]{2,1,0:T(1,128)S(1)}, u32[]{:S(2)}, u32[]{:S(2)}) collective-permute-start(f32[2,1,32]{2,1,0:T(1,128)S(1)} %broadcast.278), channel_id=1, source_target_pairs={{0,16},{16,32},{32,48},{48,64},{64,80},{80,96},{96,112},{112,128},... | collective-permute-start | bytes 776 | tf_op jit(solution)/shard_map/ppermute | solution.py:21
  12.3 32.0 %collective-permute-start.37 = (f32[2,1,32]{2,1,0:T(1,128)S(1)}, f32[2,1,32]{2,1,0:T(1,128)S(1)}, u32[]{:S(2)}, u32[]{:S(2)}) collective-permute-start(f32[2,1,32]{2,1,0:T(1,128)S(1)} %broadcast.278), channel_id=1, source_target_pairs={{16,0},{32,16},{48,32},{64,48},{80,64},{96,80},{112,96},{128,112},... | collective-permute-start | bytes 776 | tf_op jit(solution)/shard_map/ppermute | solution.py:22
  18.1 16.2 %all-to-all-start.1 = ((s32[16,1,2]{2,1,0:T(1,128)}), s32[16,1,2]{2,1,0:T(1,128)S(1)}, u32[]{:S(2)}, u32[]{:S(2)}) async-start(s32[16,1,2]{2,1,0:T(1,128)} %bitcast.2), calls=%async_computation.1 | async-start | bytes 16384 | tf_op jit(solution)/shard_map/all_to_all | solution.py:127
  24.6 22.6 %collective-permute-start.20 = (f32[4,1,64]{2,1,0:T(1,128)S(1)}, f32[4,1,64]{2,1,0:T(1,128)S(1)}, u32[]{:S(2)}, u32[]{:S(2)}) collective-permute-start(f32[4,1,64]{2,1,0:T(1,128)S(1)} %broadcast.272), channel_id=1, source_target_pairs={{0,16},{16,32},{32,48},{48,64},{64,80},{80,96},{96,112},{112,128},... | collective-permute-start | bytes 3080 | tf_op jit(solution)/shard_map/ppermute | solution.py:21
  34.2 18.4 %all-to-all-start = ((f32[16,2,8,1024]{3,2,1,0:T(8,128)}), f32[16,2,8,1024]{3,2,1,0:T(8,128)S(1)}, u32[]{:S(2)}, u32[]{:S(2)}) async-start(f32[16,2,8,1024]{3,2,1,0:T(8,128)} %bitcast.4), calls=%async_computation | async-start | bytes 2097152 | tf_op jit(solution)/shard_map/all_to_all | solution.py:126
  44.4 18.2 %collective-permute-start.38 = (f32[2,10,1]{2,1,0:T(8,128)S(1)}, f32[2,10,1]{2,1,0:T(8,128)S(1)}, u32[]{:S(2)}, u32[]{:S(2)}) collective-permute-start(f32[2,10,1]{2,1,0:T(8,128)S(1)} %get-tuple-element.173), channel_id=1, source_target_pairs={{0,1},{1,2},{2,3},{3,4},{4,5},{5,6},{6,7},{7,8},{8,9},{9,10},{10,1... | collective-permute-start | bytes 248 | tf_op jit(solution)/shard_map/ppermute | solution.py:21
  47.2 17.9 %collective-permute-start.39 = (f32[2,10,1]{2,1,0:T(8,128)S(1)}, f32[2,10,1]{2,1,0:T(8,128)S(1)}, u32[]{:S(2)}, u32[]{:S(2)}) collective-permute-start(f32[2,10,1]{2,1,0:T(8,128)S(1)} %get-tuple-element.172), channel_id=1, source_target_pairs={{1,0},{2,1},{3,2},{4,3},{5,4},{6,5},{7,6},{8,7},{9,8},{10,9},{11,1... | collective-permute-start | bytes 248 | tf_op jit(solution)/shard_map/ppermute | solution.py:22
  52.6 35.9 %all-to-all-start.2 = ((f32[16,2,8,1024]{3,2,1,0:T(8,128)}), f32[16,2,8,1024]{3,2,1,0:T(8,128)S(1)}, u32[]{:S(2)}, u32[]{:S(2)}) async-start(f32[16,2,8,1024]{3,2,1,0:T(8,128)} %bitcast.8), calls=%async_computation.2 | async-start | bytes 2097152 | tf_op jit(solution)/shard_map/all_to_all | solution.py:125
  59.8 12.4 %collective-permute-start.22 = (f32[4,18,1]{2,0,1:T(4,128)S(1)}, f32[4,18,1]{2,0,1:T(4,128)S(1)}, u32[]{:S(2)}, u32[]{:S(2)}) collective-permute-start(f32[4,18,1]{2,0,1:T(4,128)S(1)} %get-tuple-element.107), channel_id=1, source_target_pairs={{0,1},{1,2},{2,3},{3,4},{4,5},{5,6},{6,7},{7,8},{8,9},{9,10},{10,1... | collective-permute-start | bytes 872 | tf_op jit(solution)/shard_map/ppermute | solution.py:21
  62.6 12.7 %collective-permute-start.23 = (f32[4,18,1]{2,0,1:T(4,128)S(1)}, f32[4,18,1]{2,0,1:T(4,128)S(1)}, u32[]{:S(2)}, u32[]{:S(2)}) collective-permute-start(f32[4,18,1]{2,0,1:T(4,128)S(1)} %get-tuple-element.106), channel_id=1, source_target_pairs={{1,0},{2,1},{3,2},{4,3},{5,4},{6,5},{7,6},{8,7},{9,8},{10,9},{11,1... | collective-permute-start | bytes 872 | tf_op jit(solution)/shard_map/ppermute | solution.py:22
  110.6 11.2 %collective-permute-start.2 = (f32[8,34,1]{2,1,0:T(8,128)S(1)}, f32[8,34,1]{2,1,0:T(8,128)S(1)}, u32[]{:S(2)}, u32[]{:S(2)}) collective-permute-start(f32[8,34,1]{2,1,0:T(8,128)S(1)} %get-tuple-element.44), channel_id=1, source_target_pairs={{0,1},{1,2},{2,3},{3,4},{4,5},{5,6},{6,7},{7,8},{8,9},{9,10},{10,1... | collective-permute-start | bytes 3272 | tf_op jit(solution)/shard_map/ppermute | solution.py:21
  112.6 10.1 %collective-permute-start.3 = (f32[8,34,1]{2,1,0:T(8,128)S(1)}, f32[8,34,1]{2,1,0:T(8,128)S(1)}, u32[]{:S(2)}, u32[]{:S(2)}) collective-permute-start(f32[8,34,1]{2,1,0:T(8,128)S(1)} %get-tuple-element.45), channel_id=1, source_target_pairs={{1,0},{2,1},{3,2},{4,3},{5,4},{6,5},{7,6},{8,7},{9,8},{10,9},{11,1... | collective-permute-start | bytes 3272 | tf_op jit(solution)/shard_map/ppermute | solution.py:22
  116.0 13.5 %collective-permute-start.16 = (f32[4,1,64]{2,1,0:T(1,128)S(1)}, f32[4,1,64]{2,1,0:T(1,128)S(1)}, u32[]{:S(2)}, u32[]{:S(2)}) collective-permute-start(f32[4,1,64]{2,1,0:T(1,128)S(1)} %get-tuple-element.124), channel_id=1, source_target_pairs={{0,16},{16,32},{32,48},{48,64},{64,80},{80,96},{96,112},{112,128},... | collective-permute-start | bytes 3080 | tf_op jit(solution)/shard_map/ppermute | solution.py:21
  119.2 10.3 %collective-permute-start.17 = (f32[4,1,64]{2,1,0:T(1,128)S(1)}, f32[4,1,64]{2,1,0:T(1,128)S(1)}, u32[]{:S(2)}, u32[]{:S(2)}) collective-permute-start(f32[4,1,64]{2,1,0:T(1,128)S(1)} %get-tuple-element.125), channel_id=1, source_target_pairs={{16,0},{32,16},{48,32},{64,48},{80,64},{96,80},{112,96},{128,112},... | collective-permute-start | bytes 3080 | tf_op jit(solution)/shard_map/ppermute | solution.py:22
  133.8 13.2 %collective-permute-start.10 = (f32[8,34,1]{2,1,0:T(8,128)S(1)}, f32[8,34,1]{2,1,0:T(8,128)S(1)}, u32[]{:S(2)}, u32[]{:S(2)}) collective-permute-start(f32[8,34,1]{2,1,0:T(8,128)S(1)} %get-tuple-element.43), channel_id=1, source_target_pairs={{0,1},{1,2},{2,3},{3,4},{4,5},{5,6},{6,7},{7,8},{8,9},{9,10},{10,1... | collective-permute-start | bytes 3272 | tf_op jit(solution)/shard_map/ppermute | solution.py:21
  137.6 9.4 %collective-permute-start.11 = (f32[8,34,1]{2,1,0:T(8,128)S(1)}, f32[8,34,1]{2,1,0:T(8,128)S(1)}, u32[]{:S(2)}, u32[]{:S(2)}) collective-permute-start(f32[8,34,1]{2,1,0:T(8,128)S(1)} %get-tuple-element.42), channel_id=1, source_target_pairs={{1,0},{2,1},{3,2},{4,3},{5,4},{6,5},{7,6},{8,7},{9,8},{10,9},{11,1... | collective-permute-start | bytes 3272 | tf_op jit(solution)/shard_map/ppermute | solution.py:22
  139.6 12.8 %collective-permute-start.18 = (f32[4,18,1]{2,0,1:T(4,128)S(1)}, f32[4,18,1]{2,0,1:T(4,128)S(1)}, u32[]{:S(2)}, u32[]{:S(2)}) collective-permute-start(f32[4,18,1]{2,0,1:T(4,128)S(1)} %get-tuple-element.102), channel_id=1, source_target_pairs={{0,1},{1,2},{2,3},{3,4},{4,5},{5,6},{6,7},{7,8},{8,9},{9,10},{10,1... | collective-permute-start | bytes 872 | tf_op jit(solution)/shard_map/ppermute | solution.py:21
  156.7 8.3 collective-permute-start.14
  162.5 8.2 collective-permute-start.15
  185.1 12.3 %collective-permute-start.24 = (f32[4,1,64]{2,1,0:T(1,128)S(1)}, f32[4,1,64]{2,1,0:T(1,128)S(1)}, u32[]{:S(2)}, u32[]{:S(2)}) collective-permute-start(f32[4,1,64]{2,1,0:T(1,128)S(1)} %get-tuple-element.122), channel_id=1, source_target_pairs={{0,16},{16,32},{32,48},{48,64},{64,80},{80,96},{96,112},{112,128},... | collective-permute-start | bytes 3080 | tf_op jit(solution)/shard_map/ppermute | solution.py:21
  188.6 8.8 collective-permute-start.25
  190.5 12.2 %collective-permute-start.32 = (f32[2,1,32]{2,1,0:T(1,128)S(1)}, f32[2,1,32]{2,1,0:T(1,128)S(1)}, u32[]{:S(2)}, u32[]{:S(2)}) collective-permute-start(f32[2,1,32]{2,1,0:T(1,128)S(1)} %get-tuple-element.218), channel_id=1, source_target_pairs={{0,16},{16,32},{32,48},{48,64},{64,80},{80,96},{96,112},{112,128},... | collective-permute-start | bytes 776 | tf_op jit(solution)/shard_map/ppermute | solution.py:21
  206.6 13.3 %collective-permute-start.28 = (f32[4,1,64]{2,1,0:T(1,128)S(1)}, f32[4,1,64]{2,1,0:T(1,128)S(1)}, u32[]{:S(2)}, u32[]{:S(2)}) collective-permute-start(f32[4,1,64]{2,1,0:T(1,128)S(1)} %get-tuple-element.120), channel_id=1, source_target_pairs={{0,16},{16,32},{32,48},{48,64},{64,80},{80,96},{96,112},{112,128},... | collective-permute-start | bytes 3080 | tf_op jit(solution)/shard_map/ppermute | solution.py:21
  214.6 11.4 %collective-permute-start.34 = (f32[2,10,1]{2,1,0:T(8,128)S(1)}, f32[2,10,1]{2,1,0:T(8,128)S(1)}, u32[]{:S(2)}, u32[]{:S(2)}) collective-permute-start(f32[2,10,1]{2,1,0:T(8,128)S(1)} %get-tuple-element.170), channel_id=1, source_target_pairs={{0,1},{1,2},{2,3},{3,4},{4,5},{5,6},{6,7},{7,8},{8,9},{9,10},{10,1... | collective-permute-start | bytes 248 | tf_op jit(solution)/shard_map/ppermute | solution.py:21
  216.5 9.5 %collective-permute-start.35 = (f32[2,10,1]{2,1,0:T(8,128)S(1)}, f32[2,10,1]{2,1,0:T(8,128)S(1)}, u32[]{:S(2)}, u32[]{:S(2)}) collective-permute-start(f32[2,10,1]{2,1,0:T(8,128)S(1)} %get-tuple-element.171), channel_id=1, source_target_pairs={{1,0},{2,1},{3,2},{4,3},{5,4},{6,5},{7,6},{8,7},{9,8},{10,9},{11,1... | collective-permute-start | bytes 248 | tf_op jit(solution)/shard_map/ppermute | solution.py:22
  232.7 8.5 collective-permute-start.40
  514.2 8.2 collective-permute-start.99
  534.2 8.2 collective-permute-start.103
  554.3 8.2 collective-permute-start.107
  574.4 8.2 collective-permute-start.111
  (171 other events, 1540.9 us)
where the time goes:
time: 936 us; the launch traced here: 923 us
  starting transfers between devices  507 us (54%)
  waiting for transfers between devices  314 us (34%)
  local copies, waits for them, and re-layouts  62.9 us (7%)
  other arithmetic  34.7 us (4%)
    ppermute x90, waiting for transfers between devices, padded_2(): after = lax.ppermute(first, axis, down)  295 us
    ppermute x90, starting transfers between devices, padded_2(): before = lax.ppermute(last, axis, up)  257 us
    ppermute x90, starting transfers between devices, padded_2(): after = lax.ppermute(first, axis, down)  231 us
    reshape x4, local copies, waits for them, and re-layouts, restrict_mean(): field.reshape(extent[0] // 2, 2, extent[1] // 2, 2, extent[2] // 2, 2)  21.6 us
  transfers between devices with their start and end apart: 183, of which 89 were waited for; matrix products, arithmetic and copies ran while one was open for 2% of the time, Pallas kernels for 0%

commit v1 on v0

v1 whole, which is shorter than its diff:
```python
import functools

import jax
import jax.numpy as jnp
from jax import lax
from jax.experimental import pallas as pl
from jax.experimental.pallas import tpu as pltpu
from jax.sharding import PartitionSpec as P

MESH = pl.DeviceIdType.MESH
F32 = jnp.float32
I32 = jnp.int32
CYCLES = 2
BOTTOM = 6
SIDE = [(dx, dy) for dx in (-2, -1, 0, 1, 2) for dy in (-1, 0, 1) if (dx, dy) != (0, 0)]


def iota(shape, dim):
    return lax.broadcasted_iota(I32, shape, dim)


def turn(x, shift, axis):
    return pltpu.roll(x, shift % x.shape[axis], axis)


def split3(x):
    high = x.astype(jnp.bfloat16).astype(F32)
    rest = x - high
    middle = rest.astype(jnp.bfloat16).astype(F32)
    return high, middle, rest - middle


def kernel(
    nx, ny, slots_ref, table_ref, rho_hbm, rhs_hbm, out_ref,
    rho_in, rhs_in, rho_out, rhs_out, rho_got, rhs_got, tables,
    beta, source, phi_a, phi_b, wx, wy, wz, inv, diag,
    strips, strips_got,
    beta1, g1, v1, wx1, wy1, wz1, inv1, diag1,
    pairs, tiles, tiles_got, spread, gather, wide,
    in_sem, send_sem, recv_sem,
):
    gx, gy = lax.axis_index("gx"), lax.axis_index("gy")
    ky = 4 if ny % 4 == 0 else ny
    kx = ny // ky

    def beside(dx, dy):
        return (lax.rem(gx + (dx + nx), nx), lax.rem(gy + (dy + ny), ny))

    def mate(o):
        return lax.rem(gy // ky + o // ky, kx) * ky + lax.rem(gy % ky + o % ky, ky)

    used = [0]

    def send(src, dst, device):
        k = used[0]
        used[0] += 1
        copy = pltpu.make_async_remote_copy(
            src_ref=src, dst_ref=dst, send_sem=send_sem.at[k], recv_sem=recv_sem.at[k],
            device_id=device, device_id_type=MESH,
        )
        copy.start()
        return copy

    loads = [
        pltpu.make_async_copy(rho_hbm, rho_in, in_sem.at[0]),
        pltpu.make_async_copy(rhs_hbm, rhs_in, in_sem.at[1]),
    ]
    for load in loads:
        load.start()

    barrier = pltpu.get_barrier_semaphore()
    peers = [(gx, mate(o)) for o in range(1, ny)] + [beside(dx, dy) for dx, dy in SIDE if dx != 0]
    for device in peers:
        pl.semaphore_signal(barrier, inc=1, device_id=device, device_id_type=MESH)
    pl.semaphore_wait(barrier, len(peers))

    order = sorted(range(1, ny), key=lambda o: (min(o // ky, kx - o // ky) + min(o % ky, ky - o % ky), o))
    table_copies = [send(table_ref, tables.at[o], (gx, mate(o))) for o in order]
    box_copies = []
    for load, held, leaving, arrived in (
        (loads[0], rho_in, rho_out, rho_got),
        (loads[1], rhs_in, rhs_out, rhs_got),
    ):
        load.wait()
        copies = []
        for o in [*order, 0]:
            d = mate(o)
            for r in range(2):
                box = held[slots_ref[2 * d + r]]
                if o == 0:
                    arrived[r] = box
                else:
                    leaving[2 * o + r] = box
            if o:
                copies.append(
                    send(leaving.at[pl.ds(2 * o, 2)], arrived.at[pl.ds(2 * o, 2)], (gx, d))
                )
        box_copies.append(copies)

    k, n = iota((128, 512), 0), iota((128, 512), 1)
    lane = n % 256
    place = jnp.where(lane < 192, lane // 4 + 16, lane // 4 - 48)
    spread[...] = jnp.where((k // 64 == n // 256) & (k % 64 == place), 1.0, 0.0).astype(jnp.bfloat16)
    k, n = iota((256, 128), 0), iota((256, 128), 1)
    lane = k % 128
    hit = (k // 128 == n // 64) & (lane % 2 == 0) & (lane // 4 + 16 == n % 64)
    gather[...] = jnp.where(hit, 0.125, 0.0).astype(jnp.bfloat16)
    nothing = jnp.zeros((8, 256), F32)
    for ref, last in ((beta, 65), (source, 65), (wx, 65), (beta1, 33), (wx1, 33)):
        ref[0] = nothing
        ref[last] = nothing
    for ref, last in ((phi_a, 61), (v1, 29)):
        ref[4] = nothing
        ref[last] = nothing

    lanes128 = iota((8, 128), 1)
    sub, lane256 = iota((8, 256), 0), iota((8, 256), 1)

    tables[0] = table_ref[...]
    for copy in table_copies:
        copy.wait()
    owners, ids = tables[:, 0, :], tables[:, 1, :]
    mine = owners == gy
    slot = iota((ny, 128), 1)
    first = jnp.min(jnp.where(mine, slot, 128), axis=1, keepdims=True)
    index = 2 * iota((ny, 128), 0) + jnp.where(slot == first, 0, 1)
    where_from = [jnp.max(jnp.where(mine & (ids == b), index, 0)) for b in range(4)]

    def assemble(arrived, field, invert):
        for g in range(8):
            parts = [arrived[where_from[b], :, 128 * g : 128 * g + 128] for b in range(4)]
            for r in range(4):
                row = parts[0] if r == 0 else turn(parts[0], -32 * r, 1)
                for b in range(1, 4):
                    moved = parts[b] if b == r else turn(parts[b], 32 * (b - r), 1)
                    row = jnp.where(lanes128 >= 32 * b, moved, row)
                if invert:
                    row = 1.0 / row
                field[17 + 4 * g + r, :, 0:128] = row

    def exchange(which, field):
        left, right = strips.at[which, 0], strips.at[which, 1]
        from_left, from_right = strips_got.at[which, 0], strips_got.at[which, 1]
        main = pl.ds(0, 128)
        copies = [
            send(field.at[pl.ds(33, 16), :, main], field.at[pl.ds(1, 16), :, main], beside(1, 0)),
            send(field.at[pl.ds(17, 16), :, main], field.at[pl.ds(49, 16), :, main], beside(-1, 0)),
        ]

        def pack(j, carry):
            low = high = None
            for q in range(8):
                row = field[17 + 8 * j + q, :, 0:128]
                a, b = turn(row, 16 * q, 1), turn(row, 16 * q - 112, 1)
                low = a if q == 0 else jnp.where(lanes128 >= 16 * q, a, low)
                high = b if q == 0 else jnp.where(lanes128 >= 16 * q, b, high)
            left[j] = low
            right[j] = high
            return carry

        lax.fori_loop(0, 4, pack, 0)
        for dy, src, dst in ((1, right, from_left), (-1, left, from_right)):
            copies.append(send(src, dst.at[pl.ds(2, 4)], beside(0, dy)))
            copies.append(send(src.at[pl.ds(2, 2)], dst.at[pl.ds(0, 2)], beside(1, dy)))
            copies.append(send(src.at[pl.ds(0, 2)], dst.at[pl.ds(6, 2)], beside(-1, dy)))
        return copies

    row_low, row_high = jnp.where(gx > 0, 1.0, 0.0), jnp.where(gx < nx - 1, 1.0, 0.0)
    lane_low, lane_high = jnp.where(gy > 0, 1.0, 0.0), jnp.where(gy < ny - 1, 1.0, 0.0)
    in_high = lanes128 < 16
    in_low = lanes128 >= 112

    def fill(which, field, edges):
        from_left, from_right = strips_got.at[which, 0], strips_got.at[which, 1]
        scale = jnp.where(in_high, lane_high, lane_low)

        def unpack(j, carry):
            a, b = from_left[j], from_right[j]
            if edges:
                row_scale = jnp.where(j < 2, row_low, jnp.where(j < 6, 1.0, row_high))
                row_scales = scale * row_scale
            for q in range(8):
                low, high = turn(a, 112 - 16 * q, 1), turn(b, -16 * q, 1)
                both = jnp.where(in_high, high, jnp.where(in_low, low, 0.0))
                e = 1 + 8 * j + q
                if edges:
                    both = both * row_scales
                    field[e, :, 0:128] = field[e, :, 0:128] * row_scale
                field[e, :, 128:256] = both
            return carry

        lax.fori_loop(0, 8, unpack, 0)

    def blocks(low, count, step, body):
        def run(i, carry):
            body(low + step * i)
            return carry

        lax.fori_loop(0, count // step, run, 0)

    def make_weights(b_ref, refs, count, step, sh, scale):
        rx, ry, rz, ri, rd = refs
        half = 0.5 * scale
        top, bottom = sub < 8 - sh, sub >= sh

        def body(e):
            rows = [b_ref[e - 1 + k] for k in range(step + 2)]
            for k in range(step):
                b = rows[k + 1]
                east = half * (b + rows[k + 2])
                west = half * (rows[k] + b)
                north = half * (b + turn(b, -sh, 1))
                above = half * (b + jnp.where(top, turn(b, -sh, 0), 0.0))
                below = half * (b + jnp.where(bottom, turn(b, sh, 0), 0.0))
                total = east + west + north + turn(north, sh, 1) + above + below
                inside = b > 0.0
                rx[e + k] = east
                ry[e + k] = north
                rz[e + k] = jnp.where(top, above, 0.0)
                rd[e + k] = total
                ri[e + k] = jnp.where(inside, 1.0 / jnp.where(inside, total, 1.0), 0.0)

        blocks(1, count, step, body)

    def neighbours(rows, k, e, refs, sh, wests):
        rx, ry, rz = refs[:3]
        v = rows[k + 1]
        east, north, up = rx[e + k], ry[e + k], rz[e + k]
        west = rx[e - 1] if k == 0 else wests[0]
        wests[0] = east
        total = east * rows[k + 2] + west * rows[k]
        total = total + north * turn(v, -sh, 1) + turn(north * v, sh, 1)
        return total + (up * turn(v, -sh, 0) + turn(up * v, sh, 0))

    def even(sh):
        return (sub // sh + lane256 // sh) % 2 == 0

    def colour_step(v_ref, g_ref, refs, colour, low, count, step, sh, store=None):
        ri = refs[3]
        mask_even = even(sh)
        mask_odd = jnp.logical_not(mask_even)

        def body(e):
            rows = [v_ref[e - 1 + k] for k in range(step + 2)]
            wests = [None]
            for k in range(step):
                new = (g_ref[e + k] + neighbours(rows, k, e, refs, sh, wests)) * ri[e + k]
                mask = mask_even if (low + k + 1 + colour) % 2 == 0 else mask_odd
                new = jnp.where(mask, new, rows[k + 1])
                if store is None:
                    v_ref[e + k] = new
                else:
                    store(e + k, new)

        blocks(low, count, step, body)

    def first_colour(v_ref, g_ref, refs, low, count, step, sh):
        ri = refs[3]
        mask_even = even(sh)
        mask_odd = jnp.logical_not(mask_even)

        def body(e):
            for k in range(step):
                mask = mask_even if (low + k + 1) % 2 == 0 else mask_odd
                v_ref[e + k] = jnp.where(mask, g_ref[e + k] * ri[e + k], 0.0)

        blocks(low, count, step, body)

    def residual_rows(v_ref, g_ref, refs, e, count, sh):
        rows = [v_ref[e - 1 + k] for k in range(count + 2)]
        wests = [None]
        out = []
        for k in range(count):
            total = neighbours(rows, k, e, refs, sh, wests)
            out.append(g_ref[e + k] - (refs[4][e + k] * rows[k + 1] - total))
        return out

    sub_even, lane_even = sub % 2 == 0, lane256 % 2 == 0

    def mean8(t):
        t = t + jnp.where(sub_even, turn(t, -1, 0), turn(t, 1, 0))
        t = t + jnp.where(lane_even, turn(t, -1, 1), turn(t, 1, 1))
        return t * 0.125

    def to_tiles(which):
        a = pairs[:, 0, :] + pairs[:, 2, :]
        b = pairs[:, 4, :] + pairs[:, 6, :]
        stack = jnp.concatenate([*split3(jnp.concatenate([a, b], axis=1)), jnp.zeros((8, 256), F32)], axis=0)
        dots = jnp.dot(stack.astype(jnp.bfloat16), gather[...], preferred_element_type=F32)
        tile = (dots[0:8] + dots[8:16]) + dots[16:24]
        tiles[which, 1] = tile
        tiles[which, 2] = turn(tile, -32, 1)
        tiles[which, 0] = turn(tile, 32, 1)
        tiles_got[which, 2, 1] = tile
        return [
            send(tiles.at[which, 1 + dy], tiles_got.at[which, 2 - dx, 1 - dy], beside(dx, dy))
            for dx, dy in SIDE
        ]

    lanes64 = lanes128 % 64

    def coarse_field(which):
        rows = [
            jnp.where(
                lanes64 < 16, tiles_got[which, g, 0],
                jnp.where(lanes64 < 48, tiles_got[which, g, 1], tiles_got[which, g, 2]),
            )
            for g in range(5)
        ]
        return jnp.concatenate(rows, axis=0)

    def wait(copies):
        for copy in copies:
            copy.wait()

    fine = (wx, wy, wz, inv, diag)
    mid = (wx1, wy1, wz1, inv1, diag1)
    wait(box_copies[0])
    assemble(rho_got, beta, True)
    wait(exchange(0, beta))
    fill(0, beta, True)

    def restrict_beta(e):
        for k in range(2):
            beta1[e + k] = mean8(beta[2 * (e + k) - 1] + beta[2 * (e + k)])

    blocks(1, 32, 2, restrict_beta)

    def pair_beta(c):
        pairs[c] = beta1[9 + 2 * c, :, 0:128] + beta1[10 + 2 * c, :, 0:128]

    blocks(0, 8, 1, pair_beta)
    tile_copies = to_tiles(0)
    make_weights(beta, fine, 64, 4, 1, 1.0)
    make_weights(beta1, mid, 32, 4, 2, 0.25)
    wait(tile_copies)
    rows40, cols40 = iota((40, 128), 0), iota((40, 128), 1) % 64
    at_x, at_y = gx * 8 + rows40 - 16, gy * 32 + cols40 - 16
    in_grid = (at_x >= 0) & (at_x < 8 * nx) & (at_y >= 0) & (at_y < 32 * ny)
    b2 = jnp.where(in_grid, coarse_field(0), 0.0)
    half = 0.5 * 0.0625
    cx = half * (b2 + turn(b2, -1, 0))
    cy = half * (b2 + turn(b2, -1, 1))
    cz = half * (b2 + turn(b2, 64, 1))
    total = cx + turn(cx, 1, 0) + cy + turn(cy, 1, 1) + cz + half * b2
    inside = b2 > 0.0
    ci = jnp.where(inside, 1.0 / jnp.where(inside, total, 1.0), 0.0)
    coarse_even = (rows40 + cols40 + iota((40, 128), 1) // 64) % 2 == 0
    coarse_weights = (cx, cy, cz, ci)
    for k in range(4):
        wide[k] = coarse_weights[k]

    wait(box_copies[1])
    assemble(rhs_got, source, False)
    wait(exchange(1, source))
    fill(1, source, False)

    for cycle in range(CYCLES):
        phi = phi_a if cycle == 0 else phi_b
        if cycle == 0:
            first_colour(phi, source, fine, 5, 56, 8, 1)
        else:
            colour_step(phi, source, fine, 0, 5, 56, 8, 1)
        colour_step(phi, source, fine, 1, 5, 56, 8, 1)

        def restrict(e):
            out = residual_rows(phi, source, fine, 2 * e - 1, 4, 1)
            for k in range(2):
                g1[e + k] = mean8(out[2 * k] + out[2 * k + 1])

        blocks(5, 24, 2, restrict)
        first_colour(v1, g1, mid, 5, 24, 8, 2)
        colour_step(v1, g1, mid, 1, 5, 24, 4, 2)

        def pair_residual(c):
            out = residual_rows(v1, g1, mid, 9 + 2 * c, 2, 2)
            pairs[c] = (out[0] + out[1])[:, 0:128]

        blocks(0, 8, 1, pair_residual)
        wait(to_tiles(1 + cycle))
        g2 = coarse_field(1 + cycle)
        cx, cy, cz, ci = wide[0], wide[1], wide[2], wide[3]
        v2 = jnp.where(coarse_even, g2 * ci, 0.0)
        for step in range(1, 2 * BOTTOM):
            total = cx * turn(v2, -1, 0) + turn(cx * v2, 1, 0)
            total = total + cy * turn(v2, -1, 1) + turn(cy * v2, 1, 1)
            total = total + cz * turn(v2, 64, 1)
            new = (g2 + total) * ci
            v2 = jnp.where(coarse_even, new, v2) if step % 2 == 0 else jnp.where(coarse_even, v2, new)
        stack = jnp.concatenate(split3(v2[8:40]), axis=0)
        dots = jnp.dot(stack.astype(jnp.bfloat16), spread[...], preferred_element_type=F32)
        grown = (dots[0:32] + dots[32:64]) + dots[64:96]
        for c in range(1, 13):
            row = grown[c + 5 : c + 6]
            extra = jnp.where(sub < 4, row[:, 0:256], row[:, 256:512])
            for k in range(2):
                v1[3 + 2 * c + k] = v1[3 + 2 * c + k] + extra
        colour_step(v1, g1, mid, 0, 5, 24, 4, 2)
        colour_step(v1, g1, mid, 1, 5, 24, 4, 2)

        def prolong(e):
            for k in range(2):
                extra = v1[e + k]
                for row in (2 * (e + k) - 1, 2 * (e + k)):
                    phi[row] = phi[row] + extra

        blocks(7, 20, 2, prolong)
        colour_step(phi, source, fine, 0, 13, 40, 8, 1)
        if cycle < CYCLES - 1:

            def keep(e, value):
                phi_b[e] = value

            colour_step(phi, source, fine, 1, 17, 32, 8, 1, keep)
            wait(exchange(2, phi_b))
            fill(2, phi_b, True)
        else:

            def give(e, value):
                out_ref[e - 17] = value[:, 0:128]

            colour_step(phi, source, fine, 1, 17, 32, 8, 1, give)


def local(nx, ny, send_owner, send_box, rho_old, rhs_old):
    slots = send_owner.shape[2]
    owner, box = send_owner.reshape(slots), send_box.reshape(slots)
    match = owner[None, :] == jnp.arange(ny, dtype=I32)[:, None]
    place = jnp.arange(slots, dtype=I32)[None, :]
    first = jnp.min(jnp.where(match, place, slots - 1), axis=1)
    last = jnp.max(jnp.where(match, place, 0), axis=1)
    pick = jnp.stack([first, last], axis=1).reshape(2 * ny)
    table = jnp.pad(jnp.stack([owner, box]), ((0, 6), (0, 128 - slots)), constant_values=-1)
    depth, cells = rho_old.shape[3:]
    copies = 3 * (ny - 1) + 3 * 8 + 3 * len(SIDE)

    def vmem(*shape):
        return pltpu.VMEM(shape, F32)

    boxes = vmem(2 * ny, 8, 1024)
    scratch = [
        vmem(slots, 8, 1024), vmem(slots, 8, 1024), boxes, boxes, boxes, boxes, pltpu.VMEM((ny, 8, 128), I32),
        *[vmem(66, 8, 256)] * 9,
        vmem(3, 2, 4, 8, 128), vmem(3, 2, 8, 8, 128),
        *[vmem(34, 8, 256)] * 8,
        vmem(8, 8, 128), vmem(3, 3, 8, 128), vmem(3, 5, 3, 8, 128),
        pltpu.VMEM((128, 512), jnp.bfloat16), pltpu.VMEM((256, 128), jnp.bfloat16), vmem(4, 40, 128),
        pltpu.SemaphoreType.DMA((2,)), pltpu.SemaphoreType.DMA((copies,)), pltpu.SemaphoreType.DMA((copies,)),
    ]
    out = pl.pallas_call(
        functools.partial(kernel, nx, ny),
        out_shape=jax.ShapeDtypeStruct((32, 8, 128), F32),
        in_specs=[
            pl.BlockSpec(memory_space=pltpu.SMEM),
            pl.BlockSpec(memory_space=pltpu.VMEM),
            pl.BlockSpec(memory_space=pl.ANY),
            pl.BlockSpec(memory_space=pl.ANY),
        ],
        out_specs=pl.BlockSpec(memory_space=pltpu.VMEM),
        scratch_shapes=scratch,
        compiler_params=pltpu.CompilerParams(
            collective_id=0, has_side_effects=True, vmem_limit_bytes=40 * 1024 * 1024
        ),
        name="regrid_cycles",
    )(pick, table, rho_old.reshape(slots, depth, cells), rhs_old.reshape(slots, depth, cells))
    return out.transpose(1, 0, 2)


def solution(mesh):
    placed = (
        P("gx", "gy", None),
        P("gx", "gy", None),
        P("gx", "gy", None, None, None),
        P("gx", "gy", None, None, None),
    )
    return jax.shard_map(
        functools.partial(local, mesh.shape["gx"], mesh.shape["gy"]),
        mesh=mesh, in_specs=placed, out_specs=P(None, "gx", "gy"), check_vma=False,
    )
```

time: 936 us -> 96.3 us (0.10)
  the two profiles are of different devices: /device:TPU:125 before, /device:TPU:1 now
where the time goes in v1:
time: 96.3 us; the launch traced here: 96.2 us
  Pallas kernels  92 us (96%)
  local copies, waits for them, and re-layouts  3.97 us (4%)
    pallas_call x1, Pallas kernels, local(): pl.pallas_call(functools.partial(kernel, nx, ny), out_shape=jax.ShapeDtyp...  92 us
    unnamed x8, local copies, waits for them, and re-layouts  3.12 us

profile of v1, /device:TPU:1, one launch (start us, length us, event | category | flops | bytes accessed | tf_op | source)
XLA Modules:
  0.0 96.2 jit_solution(4442422322987062296)
XLA Ops:
  0.0 0.0 copy-start.2
  0.0 0.0 copy-start.3
  0.0 0.7 copy-done.2
  0.7 0.0 copy-done.3
  0.7 0.1 select_reduce_fusion.1
  0.8 0.1 copy.9
  0.9 0.1 reshape.10.slots_ref
  1.0 0.0 copy-start
  1.0 1.2 %copy-done = f32[1,1,32,8,1024]{4,3,2,1,0:T(8,128)S(1)} copy-done((f32[1,1,32,8,1024]{4,3,2,1,0:T(8,128)S(1)}, f32[1,1,32,8,1024]{4,3,2,1,0:T(8,128)}, u32[]{:S(2)}) %copy-start) | copy-done | bytes 1048600
  2.2 0.0 copy-start.1
  2.2 1.2 %copy-done.1 = f32[1,1,32,8,1024]{4,3,2,1,0:T(8,128)S(1)} copy-done((f32[1,1,32,8,1024]{4,3,2,1,0:T(8,128)S(1)}, f32[1,1,32,8,1024]{4,3,2,1,0:T(8,128)}, u32[]{:S(2)}) %copy-start.1) | copy-done | bytes 1048600
  3.5 92.0 %regrid_cycles.1 = f32[32,8,128]{2,1,0:T(8,128)S(1)} custom-call(s32[32]{0:T(128)S(1)} %reshape.10.slots_ref, s32[8,128]{1,0:T(8,128)S(1)} %pad.4.table_ref, f32[32,8,1024]{2,1,0:T(8,128)S(1)} %bitcast.8, f32[32,8,1024]{2,1,0:T(8,128)S(1)} %bitcast.9), custom_call_target="tpu_custom_call" | custom-call | tf_op jit(solution)/shard_map/regrid_cycles/pallas_call | solution.py:450
  95.5 0.7 copy.10
  (3 shorter events, 0.0 us)
Async XLA Ops:
  0.0 0.7 copy-start.2
  0.0 0.7 copy-start.3
  1.0 1.2 %copy-start = (f32[1,1,32,8,1024]{4,3,2,1,0:T(8,128)S(1)}, f32[1,1,32,8,1024]{4,3,2,1,0:T(8,128)}, u32[]{:S(2)}) copy-start(f32[1,1,32,8,1024]{4,3,2,1,0:T(8,128)} %param.6) | copy-start | bytes 3145732
  2.2 1.2 %copy-start.1 = (f32[1,1,32,8,1024]{4,3,2,1,0:T(8,128)S(1)}, f32[1,1,32,8,1024]{4,3,2,1,0:T(8,128)}, u32[]{:S(2)}) copy-start(f32[1,1,32,8,1024]{4,3,2,1,0:T(8,128)} %param.7) | copy-start | bytes 3145732

commit v2 on v1

--- a/solution.py
+++ b/solution.py
@@ -196,7 +196,7 @@
             body(low + step * i)
             return carry
 
-        lax.fori_loop(0, count // step, run, 0)
+        lax.fori_loop(0, count // step, run, 0, unroll=True)
 
     def make_weights(b_ref, refs, count, step, sh, scale):
         rx, ry, rz, ri, rd = refs
@@ -459,7 +459,7 @@
         out_specs=pl.BlockSpec(memory_space=pltpu.VMEM),
         scratch_shapes=scratch,
         compiler_params=pltpu.CompilerParams(
-            collective_id=0, has_side_effects=True, vmem_limit_bytes=40 * 1024 * 1024
+            collective_id=0, has_side_effects=True, vmem_limit_bytes=60 * 1024 * 1024
         ),
         name="regrid_cycles",
     )(pick, table, rho_old.reshape(slots, depth, cells), rhs_old.reshape(slots, depth, cells))

time: 96.3 us -> 85.4 us (0.89)
  Pallas kernels: 92 us -> 81.6 us
    pallas_call x1, Pallas kernels: 92 us -> 81.6 us  [local(): pl.pallas_call(functools.partial(kernel, nx, ny), out_shape=jax.ShapeDtyp...]
    unnamed x8 -> x4, local copies, waits for them, and re-layouts: 3.12 us -> 0.67 us
where the time goes in v2:
time: 85.4 us; the launch traced here: 85.3 us
  Pallas kernels  81.6 us (96%)
  local copies, waits for them, and re-layouts  3.53 us (4%)
    pallas_call x1, Pallas kernels, local(): pl.pallas_call(functools.partial(kernel, nx, ny), out_shape=jax.ShapeDtyp...  81.6 us

profile of v2, /device:TPU:1, one launch (start us, length us, event | category | flops | bytes accessed | tf_op | source)
XLA Modules:
  0.0 85.3 jit_solution(14668720613167836004)
XLA Ops:
  0.0 0.0 copy-start
  0.0 0.0 copy-start.1
  0.0 0.7 copy-done
  0.7 0.0 copy-done.1
  0.7 0.1 select_reduce_fusion.1
  0.8 0.6 pad.4.table_ref
  1.4 0.1 copy.9
  1.5 0.6 reshape.10.slots_ref
  2.1 81.6 %regrid_cycles.1 = f32[32,8,128]{2,1,0:T(8,128)} custom-call(s32[32]{0:T(128)} %reshape.10.slots_ref, s32[8,128]{1,0:T(8,128)} %pad.4.table_ref, f32[32,8,1024]{2,1,0:T(8,128)} %bitcast.8, f32[32,8,1024]{2,1,0:T(8,128)} %bitcast.9), custom_call_target="tpu_custom_call" | custom-call | tf_op jit(solution)/shard_map/regrid_cycles/pallas_call | solution.py:450
  83.7 1.6 %copy.10 = f32[8,32,128]{2,1,0:T(8,128)} copy(f32[8,32,128]{2,0,1:T(8,128)} %bitcast.10) | data formatting | bytes 262144 | tf_op jit(solution)/shard_map/transpose | solution.py:466
  (2 shorter events, 0.0 us)
Async XLA Ops:
  0.0 0.7 copy-start
  0.0 0.7 copy-start.1

commit v3 on v2

--- a/solution.py
+++ b/solution.py
@@ -31,9 +31,9 @@
 
 
 def kernel(
-    nx, ny, slots_ref, table_ref, rho_hbm, rhs_hbm, out_ref,
-    rho_in, rhs_in, rho_out, rhs_out, rho_got, rhs_got, tables,
-    beta, source, phi_a, phi_b, wx, wy, wz, inv, diag,
+    nx, ny, owner_hbm, box_hbm, rho_hbm, rhs_hbm, out_ref,
+    owner_in, box_in, table_ref, rho_in, rhs_in, rho_out, rhs_out, rho_got, rhs_got, tables,
+    beta, source, phi, wx, wy, wz, inv, diag,
     strips, strips_got,
     beta1, g1, v1, wx1, wy1, wz1, inv1, diag1,
     pairs, tiles, tiles_got, spread, gather, wide,
@@ -64,6 +64,8 @@
     loads = [
         pltpu.make_async_copy(rho_hbm, rho_in, in_sem.at[0]),
         pltpu.make_async_copy(rhs_hbm, rhs_in, in_sem.at[1]),
+        pltpu.make_async_copy(owner_hbm, owner_in, in_sem.at[2]),
+        pltpu.make_async_copy(box_hbm, box_in, in_sem.at[3]),
     ]
     for load in loads:
         load.start()
@@ -72,6 +74,18 @@
     peers = [(gx, mate(o)) for o in range(1, ny)] + [beside(dx, dy) for dx, dy in SIDE if dx != 0]
     for device in peers:
         pl.semaphore_signal(barrier, inc=1, device_id=device, device_id_type=MESH)
+    slots = owner_in.shape[2]
+    table_ref[...] = jnp.full((8, 128), -1, I32)
+    loads[2].wait()
+    loads[3].wait()
+    owner_row = owner_in[0]
+    table_ref[0:1, 0:slots] = owner_row
+    table_ref[1:2, 0:slots] = box_in[0]
+    at_slot = iota((1, slots), 1)
+    chosen = []
+    for o in range(ny):
+        hit = owner_row == mate(o)
+        chosen.append((jnp.min(jnp.where(hit, at_slot, slots - 1)), jnp.max(jnp.where(hit, at_slot, 0))))
     pl.semaphore_wait(barrier, len(peers))
 
     order = sorted(range(1, ny), key=lambda o: (min(o // ky, kx - o // ky) + min(o % ky, ky - o % ky), o))
@@ -86,7 +100,7 @@
         for o in [*order, 0]:
             d = mate(o)
             for r in range(2):
-                box = held[slots_ref[2 * d + r]]
+                box = held[chosen[o][r]]
                 if o == 0:
                     arrived[r] = box
                 else:
@@ -106,11 +120,8 @@
     hit = (k // 128 == n // 64) & (lane % 2 == 0) & (lane // 4 + 16 == n % 64)
     gather[...] = jnp.where(hit, 0.125, 0.0).astype(jnp.bfloat16)
     nothing = jnp.zeros((8, 256), F32)
-    for ref, last in ((beta, 65), (source, 65), (wx, 65), (beta1, 33), (wx1, 33)):
+    for ref, last in ((beta, 81), (beta1, 41)):
         ref[0] = nothing
-        ref[last] = nothing
-    for ref, last in ((phi_a, 61), (v1, 29)):
-        ref[4] = nothing
         ref[last] = nothing
 
     lanes128 = iota((8, 128), 1)
@@ -136,74 +147,63 @@
                     row = jnp.where(lanes128 >= 32 * b, moved, row)
                 if invert:
                     row = 1.0 / row
-                field[17 + 4 * g + r, :, 0:128] = row
+                field[25 + 4 * g + r, :, 0:128] = row
 
     def exchange(which, field):
         left, right = strips.at[which, 0], strips.at[which, 1]
         from_left, from_right = strips_got.at[which, 0], strips_got.at[which, 1]
         main = pl.ds(0, 128)
         copies = [
-            send(field.at[pl.ds(33, 16), :, main], field.at[pl.ds(1, 16), :, main], beside(1, 0)),
-            send(field.at[pl.ds(17, 16), :, main], field.at[pl.ds(49, 16), :, main], beside(-1, 0)),
+            send(field.at[pl.ds(33, 24), :, main], field.at[pl.ds(1, 24), :, main], beside(1, 0)),
+            send(field.at[pl.ds(25, 24), :, main], field.at[pl.ds(57, 24), :, main], beside(-1, 0)),
         ]
-
-        def pack(j, carry):
+        for j in range(8):
             low = high = None
-            for q in range(8):
-                row = field[17 + 8 * j + q, :, 0:128]
-                a, b = turn(row, 16 * q, 1), turn(row, 16 * q - 112, 1)
-                low = a if q == 0 else jnp.where(lanes128 >= 16 * q, a, low)
-                high = b if q == 0 else jnp.where(lanes128 >= 16 * q, b, high)
+            for q in range(4):
+                row = field[25 + 4 * j + q, :, 0:128]
+                a, b = turn(row, 32 * q, 1), turn(row, 32 * q - 96, 1)
+                low = a if q == 0 else jnp.where(lanes128 >= 32 * q, a, low)
+                high = b if q == 0 else jnp.where(lanes128 >= 32 * q, b, high)
             left[j] = low
             right[j] = high
-            return carry
-
-        lax.fori_loop(0, 4, pack, 0)
         for dy, src, dst in ((1, right, from_left), (-1, left, from_right)):
-            copies.append(send(src, dst.at[pl.ds(2, 4)], beside(0, dy)))
-            copies.append(send(src.at[pl.ds(2, 2)], dst.at[pl.ds(0, 2)], beside(1, dy)))
-            copies.append(send(src.at[pl.ds(0, 2)], dst.at[pl.ds(6, 2)], beside(-1, dy)))
+            copies.append(send(src.at[pl.ds(2, 6)], dst.at[pl.ds(0, 6)], beside(1, dy)))
+            copies.append(send(src.at[pl.ds(0, 6)], dst.at[pl.ds(14, 6)], beside(-1, dy)))
+            copies.append(send(src, dst.at[pl.ds(6, 8)], beside(0, dy)))
         return copies
 
     row_low, row_high = jnp.where(gx > 0, 1.0, 0.0), jnp.where(gx < nx - 1, 1.0, 0.0)
     lane_low, lane_high = jnp.where(gy > 0, 1.0, 0.0), jnp.where(gy < ny - 1, 1.0, 0.0)
-    in_high = lanes128 < 16
-    in_low = lanes128 >= 112
+    in_high = lanes128 < 32
+    in_low = lanes128 >= 96
 
     def fill(which, field, edges):
         from_left, from_right = strips_got.at[which, 0], strips_got.at[which, 1]
         scale = jnp.where(in_high, lane_high, lane_low)
 
-        def unpack(j, carry):
+        for j in range(20):
             a, b = from_left[j], from_right[j]
-            if edges:
-                row_scale = jnp.where(j < 2, row_low, jnp.where(j < 6, 1.0, row_high))
-                row_scales = scale * row_scale
-            for q in range(8):
-                low, high = turn(a, 112 - 16 * q, 1), turn(b, -16 * q, 1)
+            row_scale = row_low if j < 6 else row_high if j >= 14 else 1.0
+            for q in range(4):
+                low, high = turn(a, 96 - 32 * q, 1), turn(b, -32 * q, 1)
                 both = jnp.where(in_high, high, jnp.where(in_low, low, 0.0))
-                e = 1 + 8 * j + q
+                e = 1 + 4 * j + q
                 if edges:
-                    both = both * row_scales
-                    field[e, :, 0:128] = field[e, :, 0:128] * row_scale
+                    both = both * (scale * row_scale)
+                    if not 6 <= j < 14:
+                        field[e, :, 0:128] = field[e, :, 0:128] * row_scale
                 field[e, :, 128:256] = both
-            return carry
-
-        lax.fori_loop(0, 8, unpack, 0)
 
     def blocks(low, count, step, body):
-        def run(i, carry):
-            body(low + step * i)
-            return carry
-
-        lax.fori_loop(0, count // step, run, 0, unroll=True)
+        for e in range(low, low + count, step):
+            body(e, min(step, low + count - e))
 
     def make_weights(b_ref, refs, count, step, sh, scale):
         rx, ry, rz, ri, rd = refs
         half = 0.5 * scale
         top, bottom = sub < 8 - sh, sub >= sh
 
-        def body(e):
+        def body(e, step):
             rows = [b_ref[e - 1 + k] for k in range(step + 2)]
             for k in range(step):
                 b = rows[k + 1]
@@ -240,12 +240,12 @@
         mask_even = even(sh)
         mask_odd = jnp.logical_not(mask_even)
 
-        def body(e):
+        def body(e, step):
             rows = [v_ref[e - 1 + k] for k in range(step + 2)]
             wests = [None]
             for k in range(step):
                 new = (g_ref[e + k] + neighbours(rows, k, e, refs, sh, wests)) * ri[e + k]
-                mask = mask_even if (low + k + 1 + colour) % 2 == 0 else mask_odd
+                mask = mask_even if (e + k + 1 + colour) % 2 == 0 else mask_odd
                 new = jnp.where(mask, new, rows[k + 1])
                 if store is None:
                     v_ref[e + k] = new
@@ -259,9 +259,9 @@
         mask_even = even(sh)
         mask_odd = jnp.logical_not(mask_even)
 
-        def body(e):
+        def body(e, step):
             for k in range(step):
-                mask = mask_even if (low + k + 1) % 2 == 0 else mask_odd
+                mask = mask_even if (e + k + 1) % 2 == 0 else mask_odd
                 v_ref[e + k] = jnp.where(mask, g_ref[e + k] * ri[e + k], 0.0)
 
         blocks(low, count, step, body)
@@ -313,71 +313,102 @@
         for copy in copies:
             copy.wait()
 
+    def coarse_tiles(source_of):
+        for c in range(8):
+            pairs[c] = source_of(c)
+
     fine = (wx, wy, wz, inv, diag)
     mid = (wx1, wy1, wz1, inv1, diag1)
     wait(box_copies[0])
     assemble(rho_got, beta, True)
     wait(exchange(0, beta))
     fill(0, beta, True)
-
-    def restrict_beta(e):
-        for k in range(2):
-            beta1[e + k] = mean8(beta[2 * (e + k) - 1] + beta[2 * (e + k)])
-
-    blocks(1, 32, 2, restrict_beta)
-
-    def pair_beta(c):
-        pairs[c] = beta1[9 + 2 * c, :, 0:128] + beta1[10 + 2 * c, :, 0:128]
-
-    blocks(0, 8, 1, pair_beta)
+    for e in range(1, 41):
+        beta1[e] = mean8(beta[2 * e - 1] + beta[2 * e])
+    half = 0.5 * 0.0625
+    coarse_tiles(lambda c: beta1[13 + 2 * c, :, 0:128] + beta1[14 + 2 * c, :, 0:128])
     tile_copies = to_tiles(0)
-    make_weights(beta, fine, 64, 4, 1, 1.0)
-    make_weights(beta1, mid, 32, 4, 2, 0.25)
-    wait(tile_copies)
+    quad_sub, quad_lane = sub // 2 % 2 == 0, lane256 // 2 % 2 == 0
+    top, bottom = sub < 4, sub >= 4
+    quads = []
+    for c in range(-1, 9):
+        t = beta1[13 + 2 * c] + beta1[14 + 2 * c]
+        t = t + jnp.where(quad_sub, turn(t, -2, 0), turn(t, 2, 0))
+        quads.append((t + jnp.where(quad_lane, turn(t, -2, 1), turn(t, 2, 1))) * 0.125)
+
+    def inverse_quad(c):
+        b = quads[c + 1]
+        north = half * (b + turn(b, -4, 1))
+        above = half * (b + jnp.where(top, turn(b, -4, 0), 0.0))
+        below = half * (b + jnp.where(bottom, turn(b, 4, 0), 0.0))
+        total = half * (b + quads[c + 2]) + half * (quads[c] + b) + north + turn(north, 4, 1) + above + below
+        return (2.0 / total)[:, 0:128]
+
+    coarse_tiles(inverse_quad)
+    tile_copies += to_tiles(3)
+    make_weights(beta, fine, 80, 4, 1, 1.0)
+    make_weights(beta1, mid, 40, 4, 2, 0.25)
     rows40, cols40 = iota((40, 128), 0), iota((40, 128), 1) % 64
     at_x, at_y = gx * 8 + rows40 - 16, gy * 32 + cols40 - 16
     in_grid = (at_x >= 0) & (at_x < 8 * nx) & (at_y >= 0) & (at_y < 32 * ny)
-    b2 = jnp.where(in_grid, coarse_field(0), 0.0)
-    half = 0.5 * 0.0625
-    cx = half * (b2 + turn(b2, -1, 0))
-    cy = half * (b2 + turn(b2, -1, 1))
-    cz = half * (b2 + turn(b2, 64, 1))
-    total = cx + turn(cx, 1, 0) + cy + turn(cy, 1, 1) + cz + half * b2
-    inside = b2 > 0.0
-    ci = jnp.where(inside, 1.0 / jnp.where(inside, total, 1.0), 0.0)
     coarse_even = (rows40 + cols40 + iota((40, 128), 1) // 64) % 2 == 0
-    coarse_weights = (cx, cy, cz, ci)
-    for k in range(4):
-        wide[k] = coarse_weights[k]
 
     wait(box_copies[1])
     assemble(rhs_got, source, False)
-    wait(exchange(1, source))
+    source_copies = exchange(1, source)
+    wait(tile_copies)
+    b2 = jnp.where(in_grid, coarse_field(0), 0.0)
+    wide[0] = half * (b2 + turn(b2, -1, 0))
+    wide[1] = half * (b2 + turn(b2, -1, 1))
+    wide[2] = half * (b2 + turn(b2, 64, 1))
+    wide[3] = jnp.where(in_grid, coarse_field(3), 0.0)
+    wait(source_copies)
     fill(1, source, False)
 
+    def to_mid(low, high):
+        for e in range(low + 13, high + 13):
+            out = residual_rows(phi, source, fine, 2 * e - 1, 2, 1)
+            g1[e] = mean8(out[0] + out[1])
+
+    def fine_colour(colour, low, high, cycle):
+        if cycle == 0 and colour == 0:
+            first_colour(phi, source, fine, low + 25, high - low, 8, 1)
+        else:
+            colour_step(phi, source, fine, colour, low + 25, high - low, 8, 1)
+
+    def mid_colour(colour, low, high, fresh):
+        if fresh and colour == 0:
+            first_colour(v1, g1, mid, low + 13, high - low, 8, 2)
+        else:
+            colour_step(v1, g1, mid, colour, low + 13, high - low, 8, 2)
+
     for cycle in range(CYCLES):
-        phi = phi_a if cycle == 0 else phi_b
-        if cycle == 0:
-            first_colour(phi, source, fine, 5, 56, 8, 1)
-        else:
-            colour_step(phi, source, fine, 0, 5, 56, 8, 1)
-        colour_step(phi, source, fine, 1, 5, 56, 8, 1)
-
-        def restrict(e):
-            out = residual_rows(phi, source, fine, 2 * e - 1, 4, 1)
-            for k in range(2):
-                g1[e + k] = mean8(out[2 * k] + out[2 * k + 1])
-
-        blocks(5, 24, 2, restrict)
-        first_colour(v1, g1, mid, 5, 24, 8, 2)
-        colour_step(v1, g1, mid, 1, 5, 24, 4, 2)
+        reach = 11 if cycle < CYCLES - 1 else 0
+        after = (reach + 3) // 2
+        before = after + 3
+        fine_colour(0, -6, 38, cycle)
+        fine_colour(1, -5, 37, cycle)
+        to_mid(-2, 18)
+        mid_colour(0, -2, 18, True)
+        mid_colour(1, -1, 17, True)
 
         def pair_residual(c):
-            out = residual_rows(v1, g1, mid, 9 + 2 * c, 2, 2)
-            pairs[c] = (out[0] + out[1])[:, 0:128]
-
-        blocks(0, 8, 1, pair_residual)
-        wait(to_tiles(1 + cycle))
+            out = residual_rows(v1, g1, mid, 13 + 2 * c, 2, 2)
+            return (out[0] + out[1])[:, 0:128]
+
+        coarse_tiles(pair_residual)
+        tile_copies = to_tiles(1 + cycle)
+        outer = 2 * before + 2
+        for low, high in ((-outer, -6), (38, 32 + outer)):
+            fine_colour(0, low, high, cycle)
+        for low, high in ((1 - outer, -5), (37, 31 + outer)):
+            fine_colour(1, low, high, cycle)
+        for low, high in ((-before, -2), (18, 16 + before)):
+            to_mid(low, high)
+            mid_colour(0, low, high, True)
+        for low, high in ((1 - before, -1), (17, 15 + before)):
+            mid_colour(1, low, high, True)
+        wait(tile_copies)
         g2 = coarse_field(1 + cycle)
         cx, cy, cz, ci = wide[0], wide[1], wide[2], wide[3]
         v2 = jnp.where(coarse_even, g2 * ci, 0.0)
@@ -390,79 +421,60 @@
         stack = jnp.concatenate(split3(v2[8:40]), axis=0)
         dots = jnp.dot(stack.astype(jnp.bfloat16), spread[...], preferred_element_type=F32)
         grown = (dots[0:32] + dots[32:64]) + dots[64:96]
-        for c in range(1, 13):
-            row = grown[c + 5 : c + 6]
+        depth = (before + 1) // 2
+        for c in range(-depth, 8 + depth):
+            row = grown[c + 8 : c + 9]
             extra = jnp.where(sub < 4, row[:, 0:256], row[:, 256:512])
             for k in range(2):
-                v1[3 + 2 * c + k] = v1[3 + 2 * c + k] + extra
-        colour_step(v1, g1, mid, 0, 5, 24, 4, 2)
-        colour_step(v1, g1, mid, 1, 5, 24, 4, 2)
-
-        def prolong(e):
-            for k in range(2):
-                extra = v1[e + k]
-                for row in (2 * (e + k) - 1, 2 * (e + k)):
-                    phi[row] = phi[row] + extra
-
-        blocks(7, 20, 2, prolong)
-        colour_step(phi, source, fine, 0, 13, 40, 8, 1)
-        if cycle < CYCLES - 1:
-
-            def keep(e, value):
-                phi_b[e] = value
-
-            colour_step(phi, source, fine, 1, 17, 32, 8, 1, keep)
-            wait(exchange(2, phi_b))
-            fill(2, phi_b, True)
+                v1[13 + 2 * c + k] = v1[13 + 2 * c + k] + extra
+        mid_colour(0, -after - 1, 17 + after, False)
+        mid_colour(1, -after, 16 + after, False)
+        for e in range(13 - after, 29 + after):
+            extra = v1[e]
+            for row in (2 * e - 1, 2 * e):
+                phi[row] = phi[row] + extra
+        fine_colour(0, -reach - 1, 33 + reach, 1)
+        if reach:
+            fine_colour(1, -reach, 32 + reach, 1)
         else:
 
             def give(e, value):
-                out_ref[e - 17] = value[:, 0:128]
-
-            colour_step(phi, source, fine, 1, 17, 32, 8, 1, give)
+                out_ref[e - 25] = value[:, 0:128]
+
+            colour_step(phi, source, fine, 1, 25, 32, 8, 1, give)
 
 
 def local(nx, ny, send_owner, send_box, rho_old, rhs_old):
     slots = send_owner.shape[2]
-    owner, box = send_owner.reshape(slots), send_box.reshape(slots)
-    match = owner[None, :] == jnp.arange(ny, dtype=I32)[:, None]
-    place = jnp.arange(slots, dtype=I32)[None, :]
-    first = jnp.min(jnp.where(match, place, slots - 1), axis=1)
-    last = jnp.max(jnp.where(match, place, 0), axis=1)
-    pick = jnp.stack([first, last], axis=1).reshape(2 * ny)
-    table = jnp.pad(jnp.stack([owner, box]), ((0, 6), (0, 128 - slots)), constant_values=-1)
     depth, cells = rho_old.shape[3:]
-    copies = 3 * (ny - 1) + 3 * 8 + 3 * len(SIDE)
+    copies = 3 * (ny - 1) + 2 * 8 + 4 * len(SIDE)
 
     def vmem(*shape):
         return pltpu.VMEM(shape, F32)
 
     boxes = vmem(2 * ny, 8, 1024)
+    row = pltpu.VMEM((1, 1, slots), I32)
     scratch = [
+        row, row, pltpu.VMEM((8, 128), I32),
         vmem(slots, 8, 1024), vmem(slots, 8, 1024), boxes, boxes, boxes, boxes, pltpu.VMEM((ny, 8, 128), I32),
-        *[vmem(66, 8, 256)] * 9,
-        vmem(3, 2, 4, 8, 128), vmem(3, 2, 8, 8, 128),
-        *[vmem(34, 8, 256)] * 8,
-        vmem(8, 8, 128), vmem(3, 3, 8, 128), vmem(3, 5, 3, 8, 128),
+        *[vmem(82, 8, 256)] * 8,
+        vmem(2, 2, 8, 8, 128), vmem(2, 2, 20, 8, 128),
+        *[vmem(42, 8, 256)] * 8,
+        vmem(8, 8, 128), vmem(4, 3, 8, 128), vmem(4, 5, 3, 8, 128),
         pltpu.VMEM((128, 512), jnp.bfloat16), pltpu.VMEM((256, 128), jnp.bfloat16), vmem(4, 40, 128),
-        pltpu.SemaphoreType.DMA((2,)), pltpu.SemaphoreType.DMA((copies,)), pltpu.SemaphoreType.DMA((copies,)),
+        pltpu.SemaphoreType.DMA((4,)), pltpu.SemaphoreType.DMA((copies,)), pltpu.SemaphoreType.DMA((copies,)),
     ]
     out = pl.pallas_call(
         functools.partial(kernel, nx, ny),
         out_shape=jax.ShapeDtypeStruct((32, 8, 128), F32),
-        in_specs=[
-            pl.BlockSpec(memory_space=pltpu.SMEM),
-            pl.BlockSpec(memory_space=pltpu.VMEM),
-            pl.BlockSpec(memory_space=pl.ANY),
-            pl.BlockSpec(memory_space=pl.ANY),
-        ],
+        in_specs=[pl.BlockSpec(memory_space=pl.ANY)] * 4,
         out_specs=pl.BlockSpec(memory_space=pltpu.VMEM),
         scratch_shapes=scratch,
         compiler_params=pltpu.CompilerParams(
-            collective_id=0, has_side_effects=True, vmem_limit_bytes=60 * 1024 * 1024
+            collective_id=0, has_side_effects=True, vmem_limit_bytes=int(56 * 1024 * 1024)
         ),
         name="regrid_cycles",
-    )(pick, table, rho_old.reshape(slots, depth, cells), rhs_old.reshape(slots, depth, cells))
+    )(send_owner, send_box, rho_old.reshape(slots, depth, cells), rhs_old.reshape(slots, depth, cells))
     return out.transpose(1, 0, 2)
 
 

time: 85.4 us -> 75 us (0.88)
  Pallas kernels: 81.6 us -> 73.2 us
  local copies, waits for them, and re-layouts: 3.53 us -> 1.59 us
    pallas_call x1, Pallas kernels: 81.6 us -> 73.2 us  [local(): pl.pallas_call(functools.partial(kernel, nx, ny), out_shape=jax.ShapeDtyp...]
where the time goes in v3:
time: 75 us; the launch traced here: 74.8 us
  Pallas kernels  73.2 us (98%)
  local copies, waits for them, and re-layouts  1.59 us (2%)
    pallas_call x1, Pallas kernels, local(): pl.pallas_call(functools.partial(kernel, nx, ny), out_shape=jax.ShapeDtyp...  73.2 us
    transpose x1, local copies, waits for them, and re-layouts, local(): return out.transpose(1, 0, 2)  1.59 us

profile of v3, /device:TPU:1, one launch (start us, length us, event | category | flops | bytes accessed | tf_op | source)
XLA Modules:
  0.0 74.8 jit_solution(5879161271100293727)
XLA Ops:
  0.0 73.2 %regrid_cycles.1 = f32[32,8,128]{2,1,0:T(8,128)} custom-call(s32[1,1,32]{2,1,0:T(1,128)} %owner_hbm.1, s32[1,1,32]{2,1,0:T(1,128)} %box_hbm.1, f32[32,8,1024]{2,1,0:T(8,128)} %bitcast.3, f32[32,8,1024]{2,1,0:T(8,128)} %bitcast.4), custom_call_target="tpu_custom_call" | custom-call | tf_op jit(solution)/shard_map/regrid_cycles/pallas_call | solution.py:467
  73.3 1.6 %copy.5 = f32[8,32,128]{2,1,0:T(8,128)} copy(f32[8,32,128]{2,0,1:T(8,128)} %bitcast.5) | data formatting | bytes 262144 | tf_op jit(solution)/shard_map/transpose | solution.py:478

commit v4 on v3

--- a/solution.py
+++ b/solution.py
@@ -33,9 +33,8 @@
 def kernel(
     nx, ny, owner_hbm, box_hbm, rho_hbm, rhs_hbm, out_ref,
     owner_in, box_in, table_ref, rho_in, rhs_in, rho_out, rhs_out, rho_got, rhs_got, tables,
-    beta, source, phi, wx, wy, wz, inv, diag,
+    beta, source, beta1, fine, mid,
     strips, strips_got,
-    beta1, g1, v1, wx1, wy1, wz1, inv1, diag1,
     pairs, tiles, tiles_got, spread, gather, wide,
     in_sem, send_sem, recv_sem,
 ):
@@ -123,6 +122,10 @@
     for ref, last in ((beta, 81), (beta1, 41)):
         ref[0] = nothing
         ref[last] = nothing
+    phi0, phi1, source0, source1, *fine = [fine.at[k] for k in range(14)]
+    v0, v1, g0, g1, *mid = [mid.at[k] for k in range(14)]
+    v0[1] = nothing
+    v0[20] = nothing
 
     lanes128 = iota((8, 128), 1)
     sub, lane256 = iota((8, 256), 0), iota((8, 256), 1)
@@ -177,103 +180,90 @@
     in_high = lanes128 < 32
     in_low = lanes128 >= 96
 
-    def fill(which, field, edges):
+    def fill(which, field, put):
         from_left, from_right = strips_got.at[which, 0], strips_got.at[which, 1]
         scale = jnp.where(in_high, lane_high, lane_low)
-
         for j in range(20):
             a, b = from_left[j], from_right[j]
-            row_scale = row_low if j < 6 else row_high if j >= 14 else 1.0
             for q in range(4):
                 low, high = turn(a, 96 - 32 * q, 1), turn(b, -32 * q, 1)
                 both = jnp.where(in_high, high, jnp.where(in_low, low, 0.0))
-                e = 1 + 4 * j + q
-                if edges:
-                    both = both * (scale * row_scale)
-                    if not 6 <= j < 14:
-                        field[e, :, 0:128] = field[e, :, 0:128] * row_scale
-                field[e, :, 128:256] = both
-
-    def blocks(low, count, step, body):
-        for e in range(low, low + count, step):
-            body(e, min(step, low + count - e))
-
-    def make_weights(b_ref, refs, count, step, sh, scale):
-        rx, ry, rz, ri, rd = refs
+                put(1 + 4 * j + q, field[1 + 4 * j + q, :, 0:128], both)
+
+    edge = jnp.where(in_high, lane_high, lane_low)
+
+    def put_beta(e, main, both):
+        if not 25 <= e < 57:
+            row_scale = row_low if e < 25 else row_high
+            beta[e, :, 0:128] = main * row_scale
+            both = both * row_scale
+        beta[e, :, 128:256] = both * edge
+
+    even_fine, even_mid = (sub + lane256) % 2 == 0, (sub // 2 + lane256 // 2) % 2 == 0
+    held = []
+
+    def put_source(e, main, both):
+        held.append(jnp.concatenate([main, both], axis=1))
+        if len(held) == 2:
+            a, b = held
+            source0[e // 2] = jnp.where(even_fine, a, b)
+            source1[e // 2] = jnp.where(even_fine, b, a)
+            held.clear()
+
+    def make_weights(b_ref, refs, count, sh, even, scale):
+        within, x0, x1, y0, y1, z0, z1, i0, i1, d0 = refs
         half = 0.5 * scale
         top, bottom = sub < 8 - sh, sub >= sh
-
-        def body(e, step):
-            rows = [b_ref[e - 1 + k] for k in range(step + 2)]
-            for k in range(step):
-                b = rows[k + 1]
-                east = half * (b + rows[k + 2])
-                west = half * (rows[k] + b)
+        for p in range(1, count + 1):
+            rows = [b_ref[2 * p - 2 + k] for k in range(4)]
+            faces = [half * (rows[k] + rows[k + 1]) for k in range(3)]
+            norths, ups, totals, inverses = [], [], [], []
+            for k in (1, 2):
+                b = rows[k]
                 north = half * (b + turn(b, -sh, 1))
                 above = half * (b + jnp.where(top, turn(b, -sh, 0), 0.0))
                 below = half * (b + jnp.where(bottom, turn(b, sh, 0), 0.0))
-                total = east + west + north + turn(north, sh, 1) + above + below
+                total = faces[k] + faces[k - 1] + north + turn(north, sh, 1) + above + below
                 inside = b > 0.0
-                rx[e + k] = east
-                ry[e + k] = north
-                rz[e + k] = jnp.where(top, above, 0.0)
-                rd[e + k] = total
-                ri[e + k] = jnp.where(inside, 1.0 / jnp.where(inside, total, 1.0), 0.0)
-
-        blocks(1, count, step, body)
-
-    def neighbours(rows, k, e, refs, sh, wests):
-        rx, ry, rz = refs[:3]
-        v = rows[k + 1]
-        east, north, up = rx[e + k], ry[e + k], rz[e + k]
-        west = rx[e - 1] if k == 0 else wests[0]
-        wests[0] = east
-        total = east * rows[k + 2] + west * rows[k]
-        total = total + north * turn(v, -sh, 1) + turn(north * v, sh, 1)
-        return total + (up * turn(v, -sh, 0) + turn(up * v, sh, 0))
-
-    def even(sh):
-        return (sub // sh + lane256 // sh) % 2 == 0
-
-    def colour_step(v_ref, g_ref, refs, colour, low, count, step, sh, store=None):
-        ri = refs[3]
-        mask_even = even(sh)
-        mask_odd = jnp.logical_not(mask_even)
-
-        def body(e, step):
-            rows = [v_ref[e - 1 + k] for k in range(step + 2)]
-            wests = [None]
-            for k in range(step):
-                new = (g_ref[e + k] + neighbours(rows, k, e, refs, sh, wests)) * ri[e + k]
-                mask = mask_even if (e + k + 1 + colour) % 2 == 0 else mask_odd
-                new = jnp.where(mask, new, rows[k + 1])
-                if store is None:
-                    v_ref[e + k] = new
-                else:
-                    store(e + k, new)
-
-        blocks(low, count, step, body)
-
-    def first_colour(v_ref, g_ref, refs, low, count, step, sh):
-        ri = refs[3]
-        mask_even = even(sh)
-        mask_odd = jnp.logical_not(mask_even)
-
-        def body(e, step):
-            for k in range(step):
-                mask = mask_even if (e + k + 1) % 2 == 0 else mask_odd
-                v_ref[e + k] = jnp.where(mask, g_ref[e + k] * ri[e + k], 0.0)
-
-        blocks(low, count, step, body)
-
-    def residual_rows(v_ref, g_ref, refs, e, count, sh):
-        rows = [v_ref[e - 1 + k] for k in range(count + 2)]
-        wests = [None]
-        out = []
-        for k in range(count):
-            total = neighbours(rows, k, e, refs, sh, wests)
-            out.append(g_ref[e + k] - (refs[4][e + k] * rows[k + 1] - total))
-        return out
+                norths.append(north)
+                ups.append(jnp.where(top, above, 0.0))
+                totals.append(total)
+                inverses.append(jnp.where(inside, 1.0 / jnp.where(inside, total, 1.0), 0.0))
+            within[p] = faces[1]
+            x0[p] = jnp.where(even, faces[0], faces[2])
+            x1[p] = jnp.where(even, faces[2], faces[0])
+            for (a, b), first, second in ((norths, y0, y1), (ups, z0, z1), (inverses, i0, i1)):
+                first[p] = jnp.where(even, a, b)
+                second[p] = jnp.where(even, b, a)
+            d0[p] = jnp.where(even, totals[0], totals[1])
+
+    def neighbours(other, colour, p, refs, sh, even):
+        within, x0, x1, y0, y1, z0, z1 = refs[:7]
+        x, y, z = (x0, y0, z0) if colour == 0 else (x1, y1, z1)
+        y_other, z_other = (y1, z1) if colour == 0 else (y0, z0)
+        v = other[p]
+        before, after = other[p - 1], other[p + 1]
+        outside = jnp.where(even, before, after) if colour == 0 else jnp.where(even, after, before)
+        total = within[p] * v + x[p] * outside
+        total = total + (y[p] * turn(v, -sh, 1) + turn(y_other[p] * v, sh, 1))
+        return total + (z[p] * turn(v, -sh, 0) + turn(z_other[p] * v, sh, 0))
+
+    def sweep_colour(fields, sources, refs, colour, low, high, sh, even, store=None):
+        field, other = fields[colour], fields[1 - colour]
+        for p in range(low, high):
+            new = (sources[colour][p] + neighbours(other, colour, p, refs, sh, even)) * refs[7 + colour][p]
+            if store is None:
+                field[p] = new
+            else:
+                store(p, new)
+
+    def fresh_colour(fields, sources, refs, low, high):
+        for p in range(low, high):
+            fields[0][p] = sources[0][p] * refs[7][p]
+
+    def residual(fields, sources, refs, p, sh, even):
+        total = neighbours(fields[1], 0, p, refs, sh, even)
+        return sources[0][p] - (refs[9][p] * fields[0][p] - total)
 
     sub_even, lane_even = sub % 2 == 0, lane256 % 2 == 0
 
@@ -317,12 +307,10 @@
         for c in range(8):
             pairs[c] = source_of(c)
 
-    fine = (wx, wy, wz, inv, diag)
-    mid = (wx1, wy1, wz1, inv1, diag1)
     wait(box_copies[0])
     assemble(rho_got, beta, True)
     wait(exchange(0, beta))
-    fill(0, beta, True)
+    fill(0, beta, put_beta)
     for e in range(1, 41):
         beta1[e] = mean8(beta[2 * e - 1] + beta[2 * e])
     half = 0.5 * 0.0625
@@ -346,8 +334,8 @@
 
     coarse_tiles(inverse_quad)
     tile_copies += to_tiles(3)
-    make_weights(beta, fine, 80, 4, 1, 1.0)
-    make_weights(beta1, mid, 40, 4, 2, 0.25)
+    make_weights(beta, fine, 40, 1, even_fine, 1.0)
+    make_weights(beta1, mid, 20, 2, even_mid, 0.25)
     rows40, cols40 = iota((40, 128), 0), iota((40, 128), 1) % 64
     at_x, at_y = gx * 8 + rows40 - 16, gy * 32 + cols40 - 16
     in_grid = (at_x >= 0) & (at_x < 8 * nx) & (at_y >= 0) & (at_y < 32 * ny)
@@ -363,51 +351,56 @@
     wide[2] = half * (b2 + turn(b2, 64, 1))
     wide[3] = jnp.where(in_grid, coarse_field(3), 0.0)
     wait(source_copies)
-    fill(1, source, False)
+    fill(1, source, put_source)
+
+    phis, sources, vs, gs = (phi0, phi1), (source0, source1), (v0, v1), (g0, g1)
 
     def to_mid(low, high):
-        for e in range(low + 13, high + 13):
-            out = residual_rows(phi, source, fine, 2 * e - 1, 2, 1)
-            g1[e] = mean8(out[0] + out[1])
-
-    def fine_colour(colour, low, high, cycle):
-        if cycle == 0 and colour == 0:
-            first_colour(phi, source, fine, low + 25, high - low, 8, 1)
+        for p in range(low // 2 + 7, high // 2 + 7):
+            a, b = [mean8(residual(phis, sources, fine, 2 * p - 1 + k, 1, even_fine)) for k in range(2)]
+            g0[p] = jnp.where(even_mid, a, b)
+            g1[p] = jnp.where(even_mid, b, a)
+
+    def fine_colour(colour, low, high, fresh=False, store=None):
+        low, high = low // 2 + 13, high // 2 + 13
+        if fresh and colour == 0:
+            fresh_colour(phis, sources, fine, low, high)
         else:
-            colour_step(phi, source, fine, colour, low + 25, high - low, 8, 1)
-
-    def mid_colour(colour, low, high, fresh):
-        if fresh and colour == 0:
-            first_colour(v1, g1, mid, low + 13, high - low, 8, 2)
+            sweep_colour(phis, sources, fine, colour, low, high, 1, even_fine, store)
+
+    def mid_colour(colour, low, high, fresh=False):
+        low, high = low // 2 + 7, high // 2 + 7
+        if fresh:
+            fresh_colour(vs, gs, mid, low, high)
         else:
-            colour_step(v1, g1, mid, colour, low + 13, high - low, 8, 2)
+            sweep_colour(vs, gs, mid, colour, low, high, 2, even_mid)
 
     for cycle in range(CYCLES):
         reach = 11 if cycle < CYCLES - 1 else 0
         after = (reach + 3) // 2
         before = after + 3
-        fine_colour(0, -6, 38, cycle)
-        fine_colour(1, -5, 37, cycle)
+        fine_colour(0, -8, 40, cycle == 0)
+        fine_colour(1, -6, 38)
         to_mid(-2, 18)
         mid_colour(0, -2, 18, True)
-        mid_colour(1, -1, 17, True)
+        mid_colour(1, -2, 18)
 
         def pair_residual(c):
-            out = residual_rows(v1, g1, mid, 13 + 2 * c, 2, 2)
-            return (out[0] + out[1])[:, 0:128]
+            return residual(vs, gs, mid, 7 + c, 2, even_mid)[:, 0:128]
 
         coarse_tiles(pair_residual)
         tile_copies = to_tiles(1 + cycle)
-        outer = 2 * before + 2
-        for low, high in ((-outer, -6), (38, 32 + outer)):
-            fine_colour(0, low, high, cycle)
-        for low, high in ((1 - outer, -5), (37, 31 + outer)):
-            fine_colour(1, low, high, cycle)
+        outer = 24 if reach else 10
+        inner = outer - 2 if reach else outer
+        for low, high in ((-outer, -8), (40, 32 + outer)):
+            fine_colour(0, low, high, cycle == 0)
+        for low, high in ((-inner, -6), (38, 32 + inner)):
+            fine_colour(1, low, high)
         for low, high in ((-before, -2), (18, 16 + before)):
             to_mid(low, high)
             mid_colour(0, low, high, True)
-        for low, high in ((1 - before, -1), (17, 15 + before)):
-            mid_colour(1, low, high, True)
+        for low, high in ((-before, 0), (16, 16 + before)):
+            mid_colour(1, low, high)
         wait(tile_copies)
         g2 = coarse_field(1 + cycle)
         cx, cy, cz, ci = wide[0], wide[1], wide[2], wide[3]
@@ -425,23 +418,27 @@
         for c in range(-depth, 8 + depth):
             row = grown[c + 8 : c + 9]
             extra = jnp.where(sub < 4, row[:, 0:256], row[:, 256:512])
-            for k in range(2):
-                v1[13 + 2 * c + k] = v1[13 + 2 * c + k] + extra
-        mid_colour(0, -after - 1, 17 + after, False)
-        mid_colour(1, -after, 16 + after, False)
-        for e in range(13 - after, 29 + after):
-            extra = v1[e]
-            for row in (2 * e - 1, 2 * e):
-                phi[row] = phi[row] + extra
-        fine_colour(0, -reach - 1, 33 + reach, 1)
+            for v in vs:
+                v[7 + c] = v[7 + c] + extra
+        mid_colour(0, -after - 1, 17 + after)
+        mid_colour(1, -after - 1, 17 + after)
+        for p in range(7 - (after + 1) // 2, 7 + (17 + after) // 2):
+            a, b = v0[p], v1[p]
+            for k, extra in ((0, jnp.where(even_mid, a, b)), (1, jnp.where(even_mid, b, a))):
+                for phi in phis:
+                    phi[2 * p - 1 + k] = phi[2 * p - 1 + k] + extra
         if reach:
-            fine_colour(1, -reach, 32 + reach, 1)
+            fine_colour(0, -reach - 1, 33 + reach)
+            fine_colour(1, -reach - 1, 33 + reach)
         else:
 
-            def give(e, value):
-                out_ref[e - 25] = value[:, 0:128]
-
-            colour_step(phi, source, fine, 1, 25, 32, 8, 1, give)
+            def give(p, value):
+                a, b = phi0[p, :, 0:128], value[:, 0:128]
+                out_ref[2 * p - 26] = jnp.where(even_fine[:, 0:128], a, b)
+                out_ref[2 * p - 25] = jnp.where(even_fine[:, 0:128], b, a)
+
+            fine_colour(0, -2, 34)
+            fine_colour(1, 0, 32, store=give)
 
 
 def local(nx, ny, send_owner, send_box, rho_old, rhs_old):
@@ -457,9 +454,8 @@
     scratch = [
         row, row, pltpu.VMEM((8, 128), I32),
         vmem(slots, 8, 1024), vmem(slots, 8, 1024), boxes, boxes, boxes, boxes, pltpu.VMEM((ny, 8, 128), I32),
-        *[vmem(82, 8, 256)] * 8,
+        vmem(82, 8, 256), vmem(82, 8, 256), vmem(42, 8, 256), vmem(14, 42, 8, 256), vmem(14, 22, 8, 256),
         vmem(2, 2, 8, 8, 128), vmem(2, 2, 20, 8, 128),
-        *[vmem(42, 8, 256)] * 8,
         vmem(8, 8, 128), vmem(4, 3, 8, 128), vmem(4, 5, 3, 8, 128),
         pltpu.VMEM((128, 512), jnp.bfloat16), pltpu.VMEM((256, 128), jnp.bfloat16), vmem(4, 40, 128),
         pltpu.SemaphoreType.DMA((4,)), pltpu.SemaphoreType.DMA((copies,)), pltpu.SemaphoreType.DMA((copies,)),

time: 75 us -> 73.3 us (0.977)
  Pallas kernels: 73.2 us -> 71.5 us
    pallas_call x1, Pallas kernels: 73.2 us -> 71.5 us  [local(): pl.pallas_call(functools.partial(kernel, nx, ny), out_shape=jax.ShapeDtyp...]
where the time goes in v4:
time: 73.3 us; the launch traced here: 73.1 us
  Pallas kernels  71.5 us (98%)
  local copies, waits for them, and re-layouts  1.59 us (2%)
    pallas_call x1, Pallas kernels, local(): pl.pallas_call(functools.partial(kernel, nx, ny), out_shape=jax.ShapeDtyp...  71.5 us
    transpose x1, local copies, waits for them, and re-layouts, local(): return out.transpose(1, 0, 2)  1.59 us

profile of v4, /device:TPU:1, one launch (start us, length us, event | category | flops | bytes accessed | tf_op | source)
XLA Modules:
  0.0 73.1 jit_solution(6121990436189474387)
XLA Ops:
  0.0 71.5 %regrid_cycles.1 = f32[32,8,128]{2,1,0:T(8,128)} custom-call(s32[1,1,32]{2,1,0:T(1,128)} %owner_hbm.1, s32[1,1,32]{2,1,0:T(1,128)} %box_hbm.1, f32[32,8,1024]{2,1,0:T(8,128)} %bitcast.3, f32[32,8,1024]{2,1,0:T(8,128)} %bitcast.4), custom_call_target="tpu_custom_call" | custom-call | tf_op jit(solution)/shard_map/regrid_cycles/pallas_call | solution.py:463
  71.6 1.6 %copy.5 = f32[8,32,128]{2,1,0:T(8,128)} copy(f32[8,32,128]{2,0,1:T(8,128)} %bitcast.5) | data formatting | bytes 262144 | tf_op jit(solution)/shard_map/transpose | solution.py:474

commit v5 on v4

--- a/solution.py
+++ b/solution.py
@@ -309,13 +309,17 @@
 
     wait(box_copies[0])
     assemble(rho_got, beta, True)
-    wait(exchange(0, beta))
+    beta_copies = exchange(0, beta)
+    wait(box_copies[1])
+    assemble(rhs_got, source, False)
+    source_copies = exchange(1, source)
+    wait(beta_copies)
     fill(0, beta, put_beta)
     for e in range(1, 41):
         beta1[e] = mean8(beta[2 * e - 1] + beta[2 * e])
     half = 0.5 * 0.0625
     coarse_tiles(lambda c: beta1[13 + 2 * c, :, 0:128] + beta1[14 + 2 * c, :, 0:128])
-    tile_copies = to_tiles(0)
+    weight_copies = to_tiles(0)
     quad_sub, quad_lane = sub // 2 % 2 == 0, lane256 // 2 % 2 == 0
     top, bottom = sub < 4, sub >= 4
     quads = []
@@ -333,23 +337,14 @@
         return (2.0 / total)[:, 0:128]
 
     coarse_tiles(inverse_quad)
-    tile_copies += to_tiles(3)
-    make_weights(beta, fine, 40, 1, even_fine, 1.0)
-    make_weights(beta1, mid, 20, 2, even_mid, 0.25)
+    weight_copies += to_tiles(3)
     rows40, cols40 = iota((40, 128), 0), iota((40, 128), 1) % 64
     at_x, at_y = gx * 8 + rows40 - 16, gy * 32 + cols40 - 16
     in_grid = (at_x >= 0) & (at_x < 8 * nx) & (at_y >= 0) & (at_y < 32 * ny)
     coarse_even = (rows40 + cols40 + iota((40, 128), 1) // 64) % 2 == 0
 
-    wait(box_copies[1])
-    assemble(rhs_got, source, False)
-    source_copies = exchange(1, source)
-    wait(tile_copies)
-    b2 = jnp.where(in_grid, coarse_field(0), 0.0)
-    wide[0] = half * (b2 + turn(b2, -1, 0))
-    wide[1] = half * (b2 + turn(b2, -1, 1))
-    wide[2] = half * (b2 + turn(b2, 64, 1))
-    wide[3] = jnp.where(in_grid, coarse_field(3), 0.0)
+    make_weights(beta, fine, 40, 1, even_fine, 1.0)
+    make_weights(beta1, mid, 20, 2, even_mid, 0.25)
     wait(source_copies)
     fill(1, source, put_source)
 
@@ -401,6 +396,13 @@
             mid_colour(0, low, high, True)
         for low, high in ((-before, 0), (16, 16 + before)):
             mid_colour(1, low, high)
+        if cycle == 0:
+            wait(weight_copies)
+            b2 = jnp.where(in_grid, coarse_field(0), 0.0)
+            wide[0] = half * (b2 + turn(b2, -1, 0))
+            wide[1] = half * (b2 + turn(b2, -1, 1))
+            wide[2] = half * (b2 + turn(b2, 64, 1))
+            wide[3] = jnp.where(in_grid, coarse_field(3), 0.0)
         wait(tile_copies)
         g2 = coarse_field(1 + cycle)
         cx, cy, cz, ci = wide[0], wide[1], wide[2], wide[3]

time: 73.3 us -> 68.1 us (0.929)
  Pallas kernels: 71.5 us -> 66.3 us
    pallas_call x1, Pallas kernels: 71.5 us -> 66.3 us  [local(): pl.pallas_call(functools.partial(kernel, nx, ny), out_shape=jax.ShapeDtyp...]
where the time goes in v5:
time: 68.1 us; the launch traced here: 67.9 us
  Pallas kernels  66.3 us (97%)
  local copies, waits for them, and re-layouts  1.59 us (2%)
    pallas_call x1, Pallas kernels, local(): pl.pallas_call(functools.partial(kernel, nx, ny), out_shape=jax.ShapeDtyp...  66.3 us
    transpose x1, local copies, waits for them, and re-layouts, local(): return out.transpose(1, 0, 2)  1.59 us

profile of v5, /device:TPU:1, one launch (start us, length us, event | category | flops | bytes accessed | tf_op | source)
XLA Modules:
  0.0 67.9 jit_solution(18028346355645692612)
XLA Ops:
  0.0 66.3 %regrid_cycles.1 = f32[32,8,128]{2,1,0:T(8,128)} custom-call(s32[1,1,32]{2,1,0:T(1,128)} %owner_hbm.1, s32[1,1,32]{2,1,0:T(1,128)} %box_hbm.1, f32[32,8,1024]{2,1,0:T(8,128)} %bitcast.3, f32[32,8,1024]{2,1,0:T(8,128)} %bitcast.4), custom_call_target="tpu_custom_call" | custom-call | tf_op jit(solution)/shard_map/regrid_cycles/pallas_call | solution.py:465
  66.3 1.6 %copy.5 = f32[8,32,128]{2,1,0:T(8,128)} copy(f32[8,32,128]{2,0,1:T(8,128)} %bitcast.5) | data formatting | bytes 262144 | tf_op jit(solution)/shard_map/transpose | solution.py:476

commit v6 on v5

--- a/solution.py
+++ b/solution.py
@@ -12,7 +12,8 @@
 I32 = jnp.int32
 CYCLES = 2
 BOTTOM = 6
-SIDE = [(dx, dy) for dx in (-2, -1, 0, 1, 2) for dy in (-1, 0, 1) if (dx, dy) != (0, 0)]
+SIDE = [(-2, -1), (2, 1), (2, -1), (-2, 1), (-1, -1), (1, 1), (1, -1), (-1, 1)]
+SIDE += [(0, -1), (0, 1), (-2, 0), (2, 0), (-1, 0), (1, 0)]
 
 
 def iota(shape, dim):
@@ -87,7 +88,7 @@
         chosen.append((jnp.min(jnp.where(hit, at_slot, slots - 1)), jnp.max(jnp.where(hit, at_slot, 0))))
     pl.semaphore_wait(barrier, len(peers))
 
-    order = sorted(range(1, ny), key=lambda o: (min(o // ky, kx - o // ky) + min(o % ky, ky - o % ky), o))
+    order = sorted(range(1, ny), key=lambda o: (-min(o // ky, kx - o // ky) - min(o % ky, ky - o % ky), o))
     table_copies = [send(table_ref, tables.at[o], (gx, mate(o))) for o in order]
     box_copies = []
     for load, held, leaving, arrived in (

time: 68.1 us -> 66.4 us (0.975)
  Pallas kernels: 66.3 us -> 64.7 us
    pallas_call x1, Pallas kernels: 66.3 us -> 64.7 us  [local(): pl.pallas_call(functools.partial(kernel, nx, ny), out_shape=jax.ShapeDtyp...]
where the time goes in v6:
time: 66.4 us; the launch traced here: 66.3 us
  Pallas kernels  64.7 us (97%)
  local copies, waits for them, and re-layouts  1.59 us (2%)
    pallas_call x1, Pallas kernels, local(): pl.pallas_call(functools.partial(kernel, nx, ny), out_shape=jax.ShapeDtyp...  64.7 us
    transpose x1, local copies, waits for them, and re-layouts, local(): return out.transpose(1, 0, 2)  1.59 us

profile of v6, /device:TPU:1, one launch (start us, length us, event | category | flops | bytes accessed | tf_op | source)
XLA Modules:
  0.0 66.3 jit_solution(12920822031492122132)
XLA Ops:
  0.0 64.7 %regrid_cycles.1 = f32[32,8,128]{2,1,0:T(8,128)} custom-call(s32[1,1,32]{2,1,0:T(1,128)} %owner_hbm.1, s32[1,1,32]{2,1,0:T(1,128)} %box_hbm.1, f32[32,8,1024]{2,1,0:T(8,128)} %bitcast.3, f32[32,8,1024]{2,1,0:T(8,128)} %bitcast.4), custom_call_target="tpu_custom_call" | custom-call | tf_op jit(solution)/shard_map/regrid_cycles/pallas_call | solution.py:466
  64.7 1.6 %copy.5 = f32[8,32,128]{2,1,0:T(8,128)} copy(f32[8,32,128]{2,0,1:T(8,128)} %bitcast.5) | data formatting | bytes 262144 | tf_op jit(solution)/shard_map/transpose | solution.py:477
